TPU v7x, 128 devices: a whole 4x4x4 slice. The times are simulated.
128 devices in a mesh: expert: 16 (over y, z), dp: 8 (over x, core).
Axes of the slice: x: 4, y: 4, z: 4, core: 2. Of those that a mesh axis runs over, the one named last changes fastest.
Arguments:
- tokens: bfloat16 [8192, 4096], P(('expert', 'dp')), may hold values from -6 to 6
- routed_expert_index: int32 [8192, 8], P(('expert', 'dp')), may hold values from 0 to 95, as said below
- routing_weight: float32 [8192, 8], P(('expert', 'dp')), may hold values from 0.05 to 1
- serving_slot_expert: int32 [128], replicated, may hold values from 0 to 95, as said below
- frozen_gate_weight: bfloat16 [128, 4096, 768], P(('expert', 'dp')), may hold values from -1 to 1, as said below
- frozen_up_weight: bfloat16 [128, 4096, 768], P(('expert', 'dp')), may hold values from -1 to 1, as said below
- frozen_down_weight: bfloat16 [128, 768, 4096], P(('expert', 'dp')), may hold values from -1 to 1, as said below
- trainer_expert_order: int32 [96], replicated, may hold values from 0 to 95, each once
- trainer_adapter_rows: bfloat16 [96, 466944], P('expert'), may hold values from -2 to 2
Outputs:
- moe_out: bfloat16 [8192, 4096], P(('expert', 'dp'))
Inputs may be any that keep to these rules, and one draw needn't show every extreme that they name: `routed_expert_index`: each token names 8 different experts. At most 8 of the 64 tokens of one device name any one expert, and one expert is named by exactly 8 tokens of every device. `serving_slot_expert`: every expert holds one or two slots, and exactly 32 experts hold two. `frozen_gate_weight`: slots that hold the same expert hold equal matrices. `frozen_up_weight`: slots that hold the same expert hold equal matrices. `frozen_down_weight`: slots that hold the same expert hold equal matrices.
All inputs are finite; a program needn't handle non-finite values.
Results may differ from a plain program's by a relative error of at most 0.0067.
Values may be sent and summed in bfloat16 or wider, within the bound.
No kernel may reach another device: no remote copies, remote signals or barrier semaphores. Data moves between devices by JAX's collectives and lax.ppermute only.
A program may use at most 192 MiB of HBM per device.

v0:
```python
import jax
import jax.numpy as jnp
from jax import lax
from jax.sharding import PartitionSpec as P

row_block = 256


def expert_row_block(
    row_segment, gate_matrix, up_matrix, down_matrix, adapter_wide_factor, adapter_narrow_factor
):
    adapter_rank_value = adapter_wide_factor.shape[1]
    reduce_factor_pair = adapter_wide_factor[:2].reshape(
        2 * adapter_rank_value, adapter_wide_factor.shape[2]
    )
    reduced_input = lax.dot_general(
        row_segment,
        reduce_factor_pair,
        (((1,), (1,)), ((), ())),
        preferred_element_type=jnp.float32,
    ).astype(jnp.bfloat16)
    gate_total = jnp.dot(row_segment, gate_matrix, preferred_element_type=jnp.float32) + jnp.dot(
        reduced_input[:, :adapter_rank_value],
        adapter_narrow_factor[0],
        preferred_element_type=jnp.float32,
    )
    up_total = jnp.dot(row_segment, up_matrix, preferred_element_type=jnp.float32) + jnp.dot(
        reduced_input[:, adapter_rank_value:],
        adapter_narrow_factor[1],
        preferred_element_type=jnp.float32,
    )
    hidden_state = (jax.nn.silu(gate_total) * up_total).astype(jnp.bfloat16)
    reduced_down_input = lax.dot_general(
        hidden_state,
        adapter_narrow_factor[2],
        (((1,), (1,)), ((), ())),
        preferred_element_type=jnp.float32,
    ).astype(jnp.bfloat16)
    projected_output = jnp.dot(
        hidden_state, down_matrix, preferred_element_type=jnp.float32
    ) + jnp.dot(reduced_down_input, adapter_wide_factor[2], preferred_element_type=jnp.float32)
    return projected_output.astype(jnp.bfloat16)


def body(
    tokens,
    routed_expert_index,
    routing_weight,
    serving_slot_expert,
    frozen_gate_weight,
    frozen_up_weight,
    frozen_down_weight,
    trainer_expert_order,
    trainer_adapter_rows,
):
    expert_count = lax.axis_size("expert")
    replica_count = lax.axis_size("dp")
    replica_index = lax.axis_index("dp")
    experts = trainer_expert_order.shape[0]
    resident_rows, packed_row_width = trainer_adapter_rows.shape
    model_dim_width = tokens.shape[1]
    hidden_unit_width = frozen_gate_weight.shape[2]
    adapter_rank_value = packed_row_width // (3 * (model_dim_width + hidden_unit_width))
    trainer_row_index = (
        jnp.zeros((experts,), jnp.int32)
        .at[trainer_expert_order]
        .set(jnp.arange(experts, dtype=jnp.int32))
    )
    wanted = trainer_row_index[serving_slot_expert]
    column_span = lax.all_to_all(
        trainer_adapter_rows, "expert", split_axis=1, concat_axis=0, tiled=True
    )
    column_needs = lax.dynamic_slice_in_dim(
        wanted.reshape(expert_count, replica_count), replica_index, 1, 1
    ).reshape(expert_count)
    packed_adapter_row = lax.all_to_all(
        column_span[column_needs], "expert", split_axis=0, concat_axis=1, tiled=True
    ).reshape(packed_row_width)
    split_offset = 3 * adapter_rank_value * model_dim_width
    adapter_wide_factor = packed_adapter_row[:split_offset].reshape(
        3, adapter_rank_value, model_dim_width
    )
    adapter_narrow_factor = packed_adapter_row[split_offset:].reshape(
        3, adapter_rank_value, hidden_unit_width
    )
    tok_rows, topk_count = routed_expert_index.shape
    slots = serving_slot_expert.shape[0]
    capacity = 16 * tok_rows // slots
    buffer_rows = slots * capacity
    slot_numbers = jnp.arange(slots, dtype=jnp.int32)
    hosts_match = serving_slot_expert[None, :] == jnp.arange(experts, dtype=jnp.int32)[:, None]
    first_slot = jnp.min(jnp.where(hosts_match, slot_numbers[None, :], slots), axis=1)
    flat_ids = routed_expert_index.reshape(-1)
    target = first_slot[flat_ids]
    target_hits = (target[:, None] == slot_numbers[None, :]).astype(jnp.int32)
    slot_place = jnp.sum(jnp.cumsum(target_hits, axis=0) * target_hits, axis=1) - 1
    sent_counts = jnp.sum(target_hits, axis=0)
    cell_index = target * capacity + slot_place
    token_of_pair = jnp.arange(tok_rows * topk_count, dtype=jnp.int32) // topk_count
    cell_token = jnp.full((buffer_rows,), tok_rows, jnp.int32).at[cell_index].set(token_of_pair)
    padded_tokens = jnp.concatenate([tokens, jnp.zeros((1, model_dim_width), jnp.bfloat16)], axis=0)
    outbox = padded_tokens[cell_token].reshape(slots, capacity, model_dim_width)
    inbox, arrived = (
        lax.all_to_all(outbox, ("expert", "dp"), split_axis=0, concat_axis=0, tiled=True),
        lax.all_to_all(
            sent_counts.astype(jnp.bfloat16).reshape(slots, 1),
            ("expert", "dp"),
            split_axis=0,
            concat_axis=0,
            tiled=True,
        ),
    )
    arrived = arrived.reshape(slots).astype(jnp.int32)
    run_ends = jnp.cumsum(arrived)
    run_starts = run_ends - arrived
    live_total = run_ends[-1]
    positions = jnp.arange(buffer_rows, dtype=jnp.int32)
    source = jnp.minimum(
        jnp.sum((run_ends[None, :] <= positions[:, None]).astype(jnp.int32), axis=1), slots - 1
    )
    within = jnp.clip(positions - run_starts[source], 0, capacity - 1)
    gathered_rows = inbox.reshape(buffer_rows, model_dim_width)[source * capacity + within]
    gate_matrix = frozen_gate_weight[0]
    up_matrix = frozen_up_weight[0]
    down_matrix = frozen_down_weight[0]

    def run_block(block_index, finished):
        offset = block_index * row_block
        row_segment = lax.dynamic_slice_in_dim(gathered_rows, offset, row_block)
        projected_output = expert_row_block(
            row_segment,
            gate_matrix,
            up_matrix,
            down_matrix,
            adapter_wide_factor,
            adapter_narrow_factor,
        )
        return lax.dynamic_update_slice_in_dim(finished, projected_output, offset, 0)

    block_total = (live_total + row_block - 1) // row_block
    results = lax.fori_loop(
        0, block_total, run_block, jnp.zeros((buffer_rows, model_dim_width), jnp.bfloat16)
    )
    back_spot = jnp.clip(
        run_starts[:, None] + jnp.arange(capacity, dtype=jnp.int32)[None, :], 0, buffer_rows - 1
    ).reshape(buffer_rows)
    returned = results[back_spot].reshape(slots, capacity, model_dim_width)
    answers = lax.all_to_all(
        returned, ("expert", "dp"), split_axis=0, concat_axis=0, tiled=True
    ).reshape(buffer_rows, model_dim_width)
    pair_rows = answers[cell_index].reshape(tok_rows, topk_count, model_dim_width)
    combined = jnp.zeros((tok_rows, model_dim_width), jnp.float32)
    for column in range(topk_count):
        combined = combined + routing_weight[:, column : column + 1] * pair_rows[
            :, column, :
        ].astype(jnp.float32)
    return combined.astype(jnp.bfloat16)


def solution(mesh):
    placed = (
        P(("expert", "dp"), None),
        P(("expert", "dp"), None),
        P(("expert", "dp"), None),
        P(),
        P(("expert", "dp"), None, None),
        P(("expert", "dp"), None, None),
        P(("expert", "dp"), None, None),
        P(),
        P("expert", None),
    )
    return jax.shard_map(
        body, mesh=mesh, in_specs=placed, out_specs=P(("expert", "dp"), None), check_vma=False
    )
```

profile of v0, /device:TPU:11, one launch (start us, length us, event | category | flops | bytes accessed | tf_op | source)
XLA Modules:
  0.0 585.6 jit_solution(11205280271067147710)
XLA Ops:
  0.0 8.0 %all-to-all-start.2 = ((bf16[6,16,29184]{2,0,1:T(8,128)(2,1)}), bf16[6,16,29184]{2,0,1:T(8,128)(2,1)}, u32[]{:S(2)}, u32[]{:S(2)}) async-start(bf16[6,16,29184]{2,0,1:T(8,128)(2,1)} %bitcast.140), calls=%async_computation.2 | async-start | bytes 14942208 | tf_op jit(solution)/shard_map/all_to_all | solution.py:70
  8.3 3.3 gather_fusion
  15.6 84.3 %all-to-all-done.2 = bf16[6,16,29184]{2,0,1:T(8,128)(2,1)} async-done(((bf16[6,16,29184]{2,0,1:T(8,128)(2,1)}), bf16[6,16,29184]{2,0,1:T(8,128)(2,1)}, u32[]{:S(2)}, u32[]{:S(2)}) %all-to-all-start.2) | async-done | bytes 5603360 | tf_op jit(solution)/shard_map/all_to_all | solution.py:70
  99.9 49.2 %all-to-all-start = ((bf16[128,1,1]{2,1,0:T(2,128)(2,1)}), bf16[128,1,1]{2,1,0:T(2,128)(2,1)S(1)}, u32[]{:S(2)}, u32[]{:S(2)}) async-start(bf16[128,1,1]{2,1,0:T(2,128)(2,1)} %copy.64), calls=%async_computation | async-start | bytes 131072 | tf_op jit(solution)/shard_map/all_to_all | solution.py:105
  149.1 6.8 %all_to_all.39 = bf16[96,29184]{1,0:T(8,128)(2,1)} reshape(bf16[16,6,29184]{2,1,0:T(8,128)(2,1)} %bitcast.24) | data formatting | bytes 11206656 | tf_op jit(solution)/shard_map/all_to_all | solution.py:70
  155.9 5.3 gather_fusion.5
  161.8 1.4 reduce.7
  164.4 7.2 %all-to-all-start.3 = ((bf16[16,2,14592]{2,1,0:T(2,128)(2,1)}), bf16[16,2,14592]{2,1,0:T(2,128)(2,1)S(1)}, u32[]{:S(2)}, u32[]{:S(2)}) async-start(bf16[16,2,14592]{2,1,0:T(2,128)(2,1)} %reshape.375), calls=%async_computation.3 | async-start | bytes 1867776 | tf_op jit(solution)/shard_map/all_to_all | solution.py:76
  172.3 2.4 scatter_custom_fusion
  174.8 7.7 %gather_fusion.1 = bf16[1024,4096]{1,0:T(8,128)(2,1)} fusion(bf16[65,4096]{1,0:T(8,128)(2,1)S(1)} %concatenate.3, s32[1024]{0:T(1024)S(1)} %fusion.41), kind=kCustom, calls=%fused_computation.1 | custom fusion | bytes 16781312 | tf_op jit(solution)/shard_map/gather | solution.py:102
  182.5 2.0 all-to-all-done.3
  185.4 10.3 %all-to-all-start.1 = ((bf16[128,8,4096]{2,1,0:T(8,128)(2,1)}), bf16[128,8,4096]{2,1,0:T(8,128)(2,1)}, u32[]{:S(2)}, u32[]{:S(2)}) async-start(bf16[128,8,4096]{2,1,0:T(8,128)(2,1)} %bitcast.138), calls=%async_computation.1 | async-start | bytes 16777216 | tf_op jit(solution)/shard_map/all_to_all | solution.py:104
  197.4 2.4 convert_reduce_fusion.2
  200.1 6.6 %gather_fusion.2 = s32[1024]{0:T(1024)S(1)} fusion(s32[128]{0:T(128)S(1)} %sub.41, s32[1024]{0:T(1024)S(1)} %broadcast_clamp_fusion.2), kind=kCustom, calls=%fused_computation.2 | custom fusion | bytes 12288 | tf_op jit(solution)/shard_map/gather | solution.py:121
  206.9 4.3 reshape.376
  211.2 5.7 reduce.3
  216.9 1.4 reshape.268
  218.3 2.4 slice.93
  221.0 79.7 %all-to-all-done.1 = bf16[128,8,4096]{2,1,0:T(8,128)(2,1)} async-done(((bf16[128,8,4096]{2,1,0:T(8,128)(2,1)}), bf16[128,8,4096]{2,1,0:T(8,128)(2,1)}, u32[]{:S(2)}, u32[]{:S(2)}) %all-to-all-start.1) | async-done | bytes 8388640 | tf_op jit(solution)/shard_map/all_to_all | solution.py:104
  300.7 19.7 %gather_fusion.3 = bf16[1024,4096]{1,0:T(8,128)(2,1)} fusion(bf16[1024,4096]{1,0:T(8,128)(2,1)} %bitcast.17, s32[1024]{0:T(1024)S(1)} %broadcast_clamp_fusion.1), kind=kCustom, calls=%fused_computation.3 | custom fusion | bytes 16781312 | tf_op jit(solution)/shard_map/gather | solution.py:122
  320.5 4.3 broadcast_in_dim.22
  324.7 83.0 %while.10 = (s32[]{:T(128)}, bf16[1024,4096]{1,0:T(8,128)(2,1)}, s32[]{:T(128)}, bf16[1024,4096]{1,0:T(8,128)(2,1)}, bf16[4096,768]{1,0:T(8,128)(2,1)}, /*index=...) while((s32[]{:T(128)}, bf16[1024,4096]{1,0:T(8,128)(2,1)}, ...), condition=%wide.region_10.11_spmd, body=%wide.region_9.10_spmd.sunk | while | flops 5074608128 | bytes 81346832 | solution.py:141
  324.8 2.5 fusion.95
  327.3 5.3 fusion.94
  333.0 3.6 fusion.93
  337.0 3.8 fusion.97
  340.8 4.7 fusion.98
  345.6 2.5 fusion.95
  348.1 5.3 fusion.94
  353.8 3.6 fusion.93
  357.8 3.8 fusion.97
  361.6 4.6 fusion.98
  366.2 2.5 fusion.95
  368.8 5.3 fusion.94
  374.5 3.6 fusion.93
  378.5 3.8 fusion.97
  382.2 4.7 fusion.98
  387.0 2.5 fusion.95
  389.5 5.3 fusion.94
  395.2 3.6 fusion.93
  399.2 3.8 fusion.97
  403.0 4.7 fusion.98
  407.7 19.5 %gather_fusion.6 = bf16[1024,4096]{1,0:T(8,128)(2,1)} fusion(bf16[1024,4096]{1,0:T(8,128)(2,1)} %get-tuple-element.53, s32[1024]{0:T(1024)S(1)} %broadcast_clamp_fusion), kind=kCustom, calls=%fused_computation.6 | custom fusion | bytes 16781312 | tf_op jit(solution)/shard_map/gather | solution.py:147
  427.2 7.7 %all-to-all-start.4 = ((bf16[128,8,4096]{2,1,0:T(8,128)(2,1)}), bf16[128,8,4096]{2,1,0:T(8,128)(2,1)}, u32[]{:S(2)}, u32[]{:S(2)}) async-start(bf16[128,8,4096]{2,1,0:T(8,128)(2,1)} %bitcast.139), calls=%async_computation.4 | async-start | bytes 16777216 | tf_op jit(solution)/shard_map/all_to_all | solution.py:148
  435.0 104.9 %all-to-all-done.4 = bf16[128,8,4096]{2,1,0:T(8,128)(2,1)} async-done(((bf16[128,8,4096]{2,1,0:T(8,128)(2,1)}), bf16[128,8,4096]{2,1,0:T(8,128)(2,1)}, u32[]{:S(2)}, u32[]{:S(2)}) %all-to-all-start.4) | async-done | bytes 8388640 | tf_op jit(solution)/shard_map/all_to_all | solution.py:148
  539.9 13.0 %gather_fusion.7 = bf16[512,4096]{1,0:T(8,128)(2,1)} fusion(bf16[1024,4096]{1,0:T(8,128)(2,1)} %bitcast.30, s32[1024]{0:T(1024)S(1)} %pad_clamp_fusion), kind=kCustom, calls=%fused_computation.7 | custom fusion | bytes 8390656 | tf_op jit(solution)/shard_map/gather | solution.py:151
  552.9 23.0 %fusion.49 = (bf16[64,1,4096]{2,1,0:T(2,128)(2,1)S(1)}, bf16[64,1,4096]{2,1,0:T(2,128)(2,1)S(1)}, bf16[64,1,4096]{2,1,0:T(2,128)(2,1)S(1)}, bf16[64,1,4096]{2,1,...) fusion(bf16[64,8,4096]{2,1,0:T(8,128)(2,1)} %bitcast.137), kind=kLoop, calls=%fused_computation.118 | loop fusion | bytes 8388608 | tf_op jit(solution)/shard_map/slice | solution.py:154
  576.0 9.4 %fusion.29 = bf16[64,4096]{1,0:T(8,128)(2,1)} fusion(bf16[64,1,4096]{2,1,0:T(2,128)(2,1)S(1)} %get-tuple-element.81, bf16[64,1,4096]{2,1,0:T(2,128)(2,1)S(1)} %get-tuple-element.75, bf16[64,1,4096]{2,1,0:T(2,128)(2,1)S(1)} %get-tuple-element.76, bf16[64,1,4096]{2,1,0:T(2,128)(2,1)S(1)} %get-tuple-element.77, bf16[64,1,4096]{2,1,0:T(2,128)(2,1)S(1)} %get-tuple-element.78, ...), kind=kLoop, calls=%fused_computation.40 | loop fusion | flops 6291456 | bytes 4720640 | tf_op jit(solution)/shard_map/convert_element_type | solution.py:157
  (122 shorter events, 12.2 us)
Async XLA Ops:
  0.0 8.0 %copy-start.4 = (s32[64,8]{0,1:T(8,128)S(1)}, s32[64,8]{0,1:T(8,128)}, u32[]{:S(2)}) copy-start(s32[64,8]{0,1:T(8,128)} %param.12) | copy-start | bytes 6148
  0.0 8.2 %copy-start.7 = (s32[128]{0:T(128)S(1)}, s32[128]{0:T(128)}, u32[]{:S(2)}) copy-start(s32[128]{0:T(128)} %param.14) | copy-start | bytes 1540
  0.0 13.1 %copy-start.6 = (s32[96]{0:T(128)S(1)}, s32[96]{0:T(128)}, u32[]{:S(2)}) copy-start(s32[96]{0:T(128)} %param.18) | copy-start | bytes 1156
  0.0 99.9 %all-to-all-start.2 = ((bf16[6,16,29184]{2,0,1:T(8,128)(2,1)}), bf16[6,16,29184]{2,0,1:T(8,128)(2,1)}, u32[]{:S(2)}, u32[]{:S(2)}) async-start(bf16[6,16,29184]{2,0,1:T(8,128)(2,1)} %bitcast.140), calls=%async_computation.2 | async-start | bytes 14942208 | tf_op jit(solution)/shard_map/all_to_all | solution.py:70
  99.9 64.5 %all-to-all-start = ((bf16[128,1,1]{2,1,0:T(2,128)(2,1)}), bf16[128,1,1]{2,1,0:T(2,128)(2,1)S(1)}, u32[]{:S(2)}, u32[]{:S(2)}) async-start(bf16[128,1,1]{2,1,0:T(2,128)(2,1)} %copy.64), calls=%async_computation | async-start | bytes 131072 | tf_op jit(solution)/shard_map/all_to_all | solution.py:105
  155.9 15.7 %copy-start.1 = (bf16[64,4096]{1,0:T(8,128)(2,1)S(1)}, bf16[64,4096]{1,0:T(8,128)(2,1)}, u32[]{:S(2)}) copy-start(bf16[64,4096]{1,0:T(8,128)(2,1)} %param.11) | copy-start | bytes 1572868
  164.4 20.1 %all-to-all-start.3 = ((bf16[16,2,14592]{2,1,0:T(2,128)(2,1)}), bf16[16,2,14592]{2,1,0:T(2,128)(2,1)S(1)}, u32[]{:S(2)}, u32[]{:S(2)}) async-start(bf16[16,2,14592]{2,1,0:T(2,128)(2,1)} %reshape.375), calls=%async_computation.3 | async-start | bytes 1867776 | tf_op jit(solution)/shard_map/all_to_all | solution.py:76
  171.7 0.6 copy-start.2
  184.5 0.9 copy-start
  185.4 115.3 %all-to-all-start.1 = ((bf16[128,8,4096]{2,1,0:T(8,128)(2,1)}), bf16[128,8,4096]{2,1,0:T(8,128)(2,1)}, u32[]{:S(2)}, u32[]{:S(2)}) async-start(bf16[128,8,4096]{2,1,0:T(8,128)(2,1)} %bitcast.138), calls=%async_computation.1 | async-start | bytes 16777216 | tf_op jit(solution)/shard_map/all_to_all | solution.py:104
  320.5 4.3 slice-start.2
  324.8 8.2 %slice-start.3 = ((s8[6291456]{0:T(1024)(128)(4,1)}), s8[4194304]{0:T(1024)(128)(4,1)S(1)}, s32[]{:S(2)}) async-start(s8[6291456]{0:T(1024)(128)(4,1)} %bitcast.159), calls=%async_computation.8 | async-start | bytes 8388608 | tf_op jit(solution)/shard_map/while
  327.3 5.7 slice-start.4
  332.7 4.3 slice-start
  333.0 4.0 slice-start.1
  345.6 8.2 %slice-start.3 = ((s8[6291456]{0:T(1024)(128)(4,1)}), s8[4194304]{0:T(1024)(128)(4,1)S(1)}, s32[]{:S(2)}) async-start(s8[6291456]{0:T(1024)(128)(4,1)} %bitcast.159), calls=%async_computation.8 | async-start | bytes 8388608 | tf_op jit(solution)/shard_map/while
  348.1 5.7 slice-start.4
  353.4 4.3 slice-start
  353.8 4.0 slice-start.1
  366.2 8.2 %slice-start.3 = ((s8[6291456]{0:T(1024)(128)(4,1)}), s8[4194304]{0:T(1024)(128)(4,1)S(1)}, s32[]{:S(2)}) async-start(s8[6291456]{0:T(1024)(128)(4,1)} %bitcast.159), calls=%async_computation.8 | async-start | bytes 8388608 | tf_op jit(solution)/shard_map/while
  368.8 5.7 slice-start.4
  374.1 4.3 slice-start
  374.5 4.0 slice-start.1
  387.0 8.2 %slice-start.3 = ((s8[6291456]{0:T(1024)(128)(4,1)}), s8[4194304]{0:T(1024)(128)(4,1)S(1)}, s32[]{:S(2)}) async-start(s8[6291456]{0:T(1024)(128)(4,1)} %bitcast.159), calls=%async_computation.8 | async-start | bytes 8388608 | tf_op jit(solution)/shard_map/while
  389.5 5.7 slice-start.4
  394.9 4.3 slice-start
  395.2 4.0 slice-start.1
  427.2 7.7 %copy-start.3 = (s32[512,1]{0,1:T(1,128)S(1)}, s32[512,1]{0,1:T(1,128)}, u32[]{:S(2)}) copy-start(s32[512,1]{0,1:T(1,128)} %copy-done.2) | copy-start | bytes 6148
  427.2 7.8 %copy-start.5 = (f32[64,8]{0,1:T(8,128)S(1)}, f32[64,8]{0,1:T(8,128)}, u32[]{:S(2)}) copy-start(f32[64,8]{0,1:T(8,128)} %param.13) | copy-start | bytes 6148
  427.2 112.7 %all-to-all-start.4 = ((bf16[128,8,4096]{2,1,0:T(8,128)(2,1)}), bf16[128,8,4096]{2,1,0:T(8,128)(2,1)}, u32[]{:S(2)}, u32[]{:S(2)}) async-start(bf16[128,8,4096]{2,1,0:T(8,128)(2,1)} %bitcast.139), calls=%async_computation.4 | async-start | bytes 16777216 | tf_op jit(solution)/shard_map/all_to_all | solution.py:148
where the time goes:
time: 595 us; the launch traced here: 586 us
  waiting for transfers between devices  271 us (46%)
  local copies, waits for them, and re-layouts  128 us (22%)
  starting transfers between devices  82.4 us (14%)
  matrix products  82.2 us (14%)
  other arithmetic  20.4 us (3%)
    all_to_all x1, waiting for transfers between devices, body(): lax.all_to_all(returned, ('expert', 'dp'), split_axis=0, concat_axis=0, t...  105 us
    all_to_all x1, waiting for transfers between devices, body(): lax.all_to_all(trainer_adapter_rows, 'expert', split_axis=1, concat_axis=...  84.3 us
    all_to_all x1, waiting for transfers between devices, body(): lax.all_to_all(outbox, ('expert', 'dp'), split_axis=0, concat_axis=0, til...  79.7 us
    all_to_all x1, starting transfers between devices, body(): lax.all_to_all(sent_counts.astype(jnp.bfloat16).reshape(slots, 1), ('expe...  49.2 us
    slice x1, local copies, waits for them, and re-layouts, body(): pair_rows[:, column, :].astype(jnp.float32)  23 us
    dot_general x4, matrix products, expert_row_block(): jnp.dot(row_segment, gate_matrix, preferred_element_type=jnp.float32)  21.4 us
    gather x1, local copies, waits for them, and re-layouts, body(): inbox.reshape(buffer_rows, model_dim_width)[source * capacity + within]  19.7 us
    gather x1, local copies, waits for them, and re-layouts, body(): returned = results[back_spot].reshape(slots, capacity, model_dim_width)  19.5 us
  transfers between devices with their start and end apart: 5, of which 4 were waited for; matrix products, arithmetic and copies ran while one was open for 9% of the time, Pallas kernels for 0%

commit v1 on v0

v1 whole, which is shorter than its diff:
```python
import functools

import jax
import jax.numpy as jnp
from jax import lax
from jax.experimental import pallas as pl
from jax.experimental.pallas import tpu as pltpu
from jax.sharding import PartitionSpec as P

bf16 = jnp.bfloat16
f32 = jnp.float32
MIB = 1 << 20

FIRST = 4
SECOND = 1
MOST = 8


def params(limit_mib):
    return pltpu.CompilerParams(vmem_limit_bytes=limit_mib * MIB)


def whole(shape):
    return pl.BlockSpec(shape, lambda *_: (0,) * len(shape))


def cut_kernel(wide_span, narrow_span, wide_total, narrow_pieces, dp_size, dp_ref, rows, out, wide_sem, narrow_sem):
    dp_index = dp_ref[0]
    copies = []
    for e in range(out.shape[0]):
        piece = e * dp_size + dp_index
        wide_at = pl.multiple_of(piece * wide_span, 128)
        narrow_at = pl.multiple_of(
            wide_total + jnp.minimum(piece, narrow_pieces - 1) * narrow_span, 128
        )
        copies.append(
            pltpu.make_async_copy(
                rows.at[:, pl.ds(wide_at, wide_span)],
                out.at[e, :, pl.ds(0, wide_span)],
                wide_sem.at[e],
            )
        )
        copies.append(
            pltpu.make_async_copy(
                rows.at[:, pl.ds(narrow_at, narrow_span)],
                out.at[e, :, pl.ds(wide_span, narrow_span)],
                narrow_sem.at[e],
            )
        )
    for copy in copies:
        copy.start()
    for copy in copies:
        copy.wait()


def cut_pieces(rows, dp_index, groups, dp_size, wide_total, wide_span, narrow_span, narrow_pieces):
    held = rows.shape[0]
    return pl.pallas_call(
        functools.partial(
            cut_kernel, wide_span, narrow_span, wide_total, narrow_pieces, dp_size
        ),
        in_specs=[
            pl.BlockSpec(memory_space=pltpu.SMEM),
            pl.BlockSpec(memory_space=pl.ANY),
        ],
        out_specs=pl.BlockSpec(memory_space=pl.ANY),
        out_shape=jax.ShapeDtypeStruct((groups, held, wide_span + narrow_span), bf16),
        scratch_shapes=[
            pltpu.SemaphoreType.DMA((groups,)),
            pltpu.SemaphoreType.DMA((groups,)),
        ],
        name="adapter_cut",
    )(dp_index.reshape(1), rows)


def pick_kernel(held, wanted, flag, pieces, out, rows):
    groups, _, span = pieces.shape
    slots = out.shape[0]
    rows[...] = jnp.zeros_like(rows)
    for e in range(groups):
        rows[8 * e : 8 * e + held, :] = pieces[e].astype(f32)
    want = wanted[...]
    place = (want // held) * 8 + want % held
    chosen = lax.broadcasted_iota(jnp.int32, (8 * groups, slots), 0) == place
    picked = lax.dot_general(
        chosen.astype(bf16),
        rows[...].astype(bf16),
        (((0,), (0,)), ((), ())),
        preferred_element_type=f32,
    )
    tail = jnp.broadcast_to(flag[...], (slots, out.shape[1] * out.shape[2] - span))
    full = jnp.concatenate([picked, tail], axis=1).astype(bf16)
    out[...] = full.reshape(out.shape)


def pick_pieces(pieces, wanted, flag, slots):
    groups, held, span = pieces.shape
    units = 32
    return pl.pallas_call(
        functools.partial(pick_kernel, held),
        out_shape=jax.ShapeDtypeStruct((slots, units, 128), bf16),
        scratch_shapes=[pltpu.VMEM((8 * groups, span), f32)],
        compiler_params=params(40),
        name="adapter_pick",
    )(wanted.reshape(1, slots), flag.reshape(1, 1), pieces)


def placement(ids, info):
    tokens = ids.shape[0]
    named = ids[:, 0:1] == info[0:1, :]
    for k in range(1, ids.shape[1]):
        named = named | (ids[:, k : k + 1] == info[0:1, :])
    before = lax.broadcasted_iota(jnp.int32, (tokens, tokens), 0) > lax.broadcasted_iota(
        jnp.int32, (tokens, tokens), 1
    )
    rank = jnp.dot(before.astype(bf16), named.astype(bf16), preferred_element_type=f32)
    return named & (rank == info[1:2, :].astype(f32))


def dispatch_kernel(ids, info, tokens, out):
    fills = placement(ids[...], info[...]).astype(bf16)
    sent = lax.dot_general(
        fills, tokens[...], (((0,), (0,)), ((), ())), preferred_element_type=f32
    )
    out[...] = sent.astype(bf16).reshape(out.shape)


def dispatch(ids, info, tokens, slots, cell):
    rows = info.shape[1]
    block = 128
    steps = rows // block
    count, width = tokens.shape
    out_block = (slots // steps,) + cell
    return pl.pallas_call(
        dispatch_kernel,
        grid=(steps,),
        in_specs=[
            whole(ids.shape),
            pl.BlockSpec((2, block), lambda i: (0, i)),
            whole(tokens.shape),
        ],
        out_specs=pl.BlockSpec(out_block, lambda i: (i, 0, 0)),
        out_shape=jax.ShapeDtypeStruct((slots,) + cell, bf16),
        compiler_params=params(32),
        cost_estimate=pl.CostEstimate(
            flops=2 * rows * count * width, bytes_accessed=2 * rows * width, transcendentals=0
        ),
        name="token_dispatch",
    )(ids, info, tokens)


def expert_kernel(
    up_steps,
    x_ref,
    gate_ref,
    up_ref,
    down_ref,
    wide,
    narrow,
    out,
    x,
    shrunk,
    hidden,
    shrunk_down,
):
    step = pl.program_id(0)
    rank = wide.shape[0] // 3
    tile = gate_ref.shape[1]

    @pl.when(step == 0)
    def _():
        x[...] = x_ref[...].reshape(x.shape)
        shrunk[...] = lax.dot_general(
            x[...],
            wide[0 : 2 * rank, :],
            (((1,), (1,)), ((), ())),
            preferred_element_type=f32,
        ).astype(bf16)

    for f in range(up_steps):

        @pl.when(step == f)
        def _():
            at = slice(f * tile, (f + 1) * tile)
            gate = jnp.dot(x[...], gate_ref[...], preferred_element_type=f32) + jnp.dot(
                shrunk[:, :rank], narrow[0:rank, at], preferred_element_type=f32
            )
            up = jnp.dot(x[...], up_ref[...], preferred_element_type=f32) + jnp.dot(
                shrunk[:, rank:], narrow[rank : 2 * rank, at], preferred_element_type=f32
            )
            hidden[:, at] = (gate / (1.0 + jnp.exp(-gate)) * up).astype(bf16)

    @pl.when(step == up_steps)
    def _():
        shrunk_down[...] = lax.dot_general(
            hidden[...],
            narrow[2 * rank :, :],
            (((1,), (1,)), ((), ())),
            preferred_element_type=f32,
        ).astype(bf16)

    @pl.when(step >= up_steps)
    def _():
        width = down_ref.shape[1]
        at = pl.multiple_of((step - up_steps) * width, width)
        total = jnp.dot(hidden[...], down_ref[...], preferred_element_type=f32) + jnp.dot(
            shrunk_down[...], wide[2 * rank :, pl.ds(at, width)], preferred_element_type=f32
        )
        out[...] = total.astype(bf16).reshape(out.shape)


def expert(x, gate, up, down, wide, narrow):
    model, units = gate.shape
    slots = x.shape[0]
    rows = x.size // model
    tile = 256
    up_steps = units // tile
    halves = x.shape[2] != model
    down_width = 1024
    down_steps = model // down_width
    rank = wide.shape[0] // 3

    def down_at(i):
        return jnp.maximum(i - up_steps, 0)

    out_rows = (rows, down_width) if halves else (slots, x.shape[1], down_width)
    out_shape = (rows, model) if halves else x.shape
    if halves:
        out_map = lambda i: (0, down_at(i))
    else:
        out_map = lambda i: (0, 0, down_at(i))
    return pl.pallas_call(
        functools.partial(expert_kernel, up_steps),
        grid=(up_steps + down_steps,),
        in_specs=[
            whole(x.shape),
            pl.BlockSpec((model, tile), lambda i: (0, jnp.minimum(i, up_steps - 1))),
            pl.BlockSpec((model, tile), lambda i: (0, jnp.minimum(i, up_steps - 1))),
            pl.BlockSpec((units, down_width), lambda i: (0, down_at(i))),
            whole(wide.shape),
            whole(narrow.shape),
        ],
        out_specs=pl.BlockSpec(out_rows, out_map),
        out_shape=jax.ShapeDtypeStruct(out_shape, bf16),
        scratch_shapes=[
            pltpu.VMEM((rows, model), bf16),
            pltpu.VMEM((rows, 2 * rank), bf16),
            pltpu.VMEM((rows, units), bf16),
            pltpu.VMEM((rows, rank), bf16),
        ],
        compiler_params=params(56),
        cost_estimate=pl.CostEstimate(
            flops=6 * rows * model * units,
            bytes_accessed=6 * model * units + 4 * rows * model,
            transcendentals=rows * units,
        ),
        name="slot_expert",
    )(x, gate, up, down, wide, narrow)


def combine_kernel(ids, weight, info, answers, *rest):
    out = rest[-1]
    fills = placement(ids[...], info[...])
    given = jnp.zeros(fills.shape, f32)
    for k in range(ids.shape[1]):
        given = given + jnp.where(ids[:, k : k + 1] == info[0:1, :], weight[:, k : k + 1], 0.0)
    given = jnp.where(fills, given, 0.0)
    high = given.astype(bf16)
    low = (given - high.astype(f32)).astype(bf16)
    both = jnp.concatenate([high, low], axis=0)
    rows = info.shape[1]
    block = answers[...].reshape(rows, out.shape[1])
    sums = jnp.dot(both, block, preferred_element_type=f32)
    count = ids.shape[0]
    total = sums[:count] + sums[count:]
    if len(rest) == 2:
        total = total + rest[0][...]
    out[...] = total.astype(out.dtype)


def combine(ids, weight, info, answers, before=None, kind=f32):
    count = ids.shape[0]
    rows = info.shape[1]
    flat = answers.ndim == 2
    model = answers.shape[-1]
    width = 1024
    if flat:
        answer_spec = pl.BlockSpec((rows, width), lambda i: (0, i))
    else:
        answer_spec = pl.BlockSpec(answers.shape[:2] + (width,), lambda i: (0, 0, i))
    total_spec = pl.BlockSpec((count, width), lambda i: (0, i))
    more = () if before is None else (before,)
    return pl.pallas_call(
        combine_kernel,
        grid=(model // width,),
        in_specs=[whole(ids.shape), whole(weight.shape), whole(info.shape), answer_spec]
        + [total_spec] * len(more),
        out_specs=total_spec,
        out_shape=jax.ShapeDtypeStruct((count, model), kind),
        compiler_params=params(32),
        cost_estimate=pl.CostEstimate(
            flops=4 * count * rows * model, bytes_accessed=2 * rows * model, transcendentals=0
        ),
        name="token_combine",
    )(ids, weight, info, answers, *more)


def body(
    tokens,
    ids,
    weight,
    serving,
    gate,
    up,
    down,
    trainer_order,
    trainer_rows,
):
    groups = lax.axis_size("expert")
    dp_size = lax.axis_size("dp")
    dp_index = lax.axis_index("dp").astype(jnp.int32)
    slots = serving.shape[0]
    experts = trainer_order.shape[0]
    held, packed = trainer_rows.shape
    count, model = tokens.shape
    units = gate.shape[2]
    rank = packed // (3 * (model + units))
    everyone = ("expert", "dp")

    slot_at = jnp.arange(slots, dtype=jnp.int32)
    same = serving[:, None] == serving[None, :]
    second = jnp.any(same & (slot_at[None, :] < slot_at[:, None]), axis=1)
    hot = jnp.sum(same.astype(jnp.int32), axis=1) > 1

    def rows_info(first, places, filled):
        place = jnp.arange(places, dtype=jnp.int32)[None, :]
        at = first + place
        ranks = jnp.where(hot[:, None], 2 * at + second[:, None].astype(jnp.int32), at)
        ranks = jnp.where(place < filled, ranks, -1)
        who = jnp.broadcast_to(serving[:, None], (slots, places))
        return jnp.stack([who.reshape(-1), ranks.reshape(-1)])

    info_a = rows_info(0, FIRST, FIRST)
    info_b = rows_info(FIRST, SECOND, SECOND)
    info_c = rows_info(FIRST + SECOND, 4, MOST - FIRST - SECOND)
    named = jnp.sum((ids.reshape(-1)[:, None] == serving[None, :]).astype(jnp.int32), axis=0)
    left_over = jnp.any((named > FIRST + SECOND) & ~hot).astype(f32)

    wide_total = 3 * rank * model
    pieces = groups * dp_size
    wide_span = wide_total // pieces
    mine = cut_pieces(
        trainer_rows, dp_index, groups, dp_size, wide_total, wide_span, units, 3 * rank
    )
    spread = lax.all_to_all(mine, "expert", split_axis=0, concat_axis=0, tiled=True)
    trainer_row = jnp.sum(
        jnp.where(
            serving[:, None] == trainer_order[None, :],
            jnp.arange(experts, dtype=jnp.int32)[None, :],
            0,
        ),
        axis=1,
    )
    picked = pick_pieces(spread, trainer_row, left_over, slots)
    factors = lax.all_to_all(picked, everyone, split_axis=0, concat_axis=0, tiled=True)
    wide_units = wide_span // 128
    span_units = (wide_span + units) // 128
    wide = factors[:, :wide_units, :].reshape(3 * rank, model)
    narrow = factors[: 3 * rank, wide_units:span_units, :].reshape(3 * rank, units)
    any_left = jnp.max(factors[:, span_units, 0].astype(f32)) > 0.0

    def there(cells):
        return lax.all_to_all(cells, everyone, split_axis=0, concat_axis=0, tiled=True)

    def run(x):
        return expert(x, gate[0], up[0], down[0], wide, narrow)

    cell_a = (FIRST, model)
    cell_b = (2, model // 2)
    in_a = there(dispatch(ids, info_a, tokens, slots, cell_a))
    in_b = there(dispatch(ids, info_b, tokens, slots, cell_b))
    back_a = there(run(in_a))
    back_b = there(run(in_b).reshape((slots,) + cell_b)).reshape(slots, model)
    total = combine(ids, weight, info_a, back_a)

    def rest():
        in_c = there(dispatch(ids, info_c, tokens, slots, cell_a))
        return combine(ids, weight, info_c, there(run(in_c)), total)

    total = lax.cond(any_left, rest, lambda: total)
    return combine(ids, weight, info_b, back_b, total, bf16)


def solution(mesh):
    split = P(("expert", "dp"), None)
    slot = P(("expert", "dp"), None, None)
    placed = (split, split, split, P(), slot, slot, slot, P(), P("expert", None))
    return jax.shard_map(body, mesh=mesh, in_specs=placed, out_specs=split, check_vma=False)
```

time: 595 us -> 262 us (0.44)
  waiting for transfers between devices: 271 us -> 113 us
  local copies, waits for them, and re-layouts: 128 us -> 8.15 us
  matrix products: 82.2 us -> 0 us
  Pallas kernels: 0 us -> 78.5 us
  starting transfers between devices: 82.4 us -> 53.3 us
  other arithmetic: 20.4 us -> 3.1 us
    all_to_all x5 -> x6, waiting for transfers between devices: 271 us -> 113 us  [the longest x4 92.4 us: there(): lax.all_to_all(cells, everyone, split_axis=0, concat_axis=0, tiled=True)]
    dot_general x28 -> x0, matrix products: 82.2 us -> none  [the longest x4 21.4 us: expert_row_block(): jnp.dot(row_segment, gate_matrix, preferred_element_type=jnp.float32)]
    pallas_call x0 -> x8, Pallas kernels: none -> 78.5 us  [the longest x2 33.3 us: expert(): pl.pallas_call(functools.partial(expert_kernel, up_steps), grid=(up_steps...]
    gather x8 -> x0, local copies, waits for them, and re-layouts: 76.5 us -> none  [the longest x1 19.7 us: body(): inbox.reshape(buffer_rows, model_dim_width)[source * capacity + within]]
    all_to_all x5 -> x6, starting transfers between devices: 82.4 us -> 53.3 us  [the longest x4 36.3 us: there(): lax.all_to_all(cells, everyone, split_axis=0, concat_axis=0, tiled=True)]
    slice x10 -> x2, local copies, waits for them, and re-layouts: 26.2 us -> 2.16 us  [the longest x1 1.22 us: body(): wide = factors[:, :wide_units, :].reshape(3 * rank, model)]
    convert_element_type x4 -> x1, other arithmetic: 11.9 us -> 0.01 us  [rows_info(): second[:, None].astype(jnp.int32)]
    all_to_all x2 -> x0, local copies, waits for them, and re-layouts: 7.39 us -> none  [the longest x1 6.8 us: body(): lax.all_to_all(trainer_adapter_rows, 'expert', split_axis=1, concat_axis=...]
  transfers between devices with their start and end apart: 5 -> 6, of which waited for: 4 -> 5; matrix products, arithmetic and copies ran while one was open for 9% -> 4% of each run, Pallas kernels for 0% -> 15%
where the time goes in v1:
time: 262 us; the launch traced here: 258 us
  waiting for transfers between devices  113 us (43%)
  Pallas kernels  78.5 us (30%)
  starting transfers between devices  53.3 us (20%)
  local copies, waits for them, and re-layouts  8.15 us (3%)
  other arithmetic  3.1 us (1%)
    all_to_all x4, waiting for transfers between devices, there(): lax.all_to_all(cells, everyone, split_axis=0, concat_axis=0, tiled=True)  92.4 us
    all_to_all x4, starting transfers between devices, there(): lax.all_to_all(cells, everyone, split_axis=0, concat_axis=0, tiled=True)  36.3 us
    pallas_call x2, Pallas kernels, expert(): pl.pallas_call(functools.partial(expert_kernel, up_steps), grid=(up_steps...  33.3 us
    pallas_call x1, Pallas kernels, cut_pieces(): pl.pallas_call(functools.partial(cut_kernel, wide_span, narrow_span, wide...  31.2 us
    all_to_all x1, waiting for transfers between devices, body(): lax.all_to_all(mine, 'expert', split_axis=0, concat_axis=0, tiled=True)  10.9 us
    all_to_all x1, waiting for transfers between devices, body(): lax.all_to_all(picked, everyone, split_axis=0, concat_axis=0, tiled=True)  9.76 us
    all_to_all x1, starting transfers between devices, body(): lax.all_to_all(picked, everyone, split_axis=0, concat_axis=0, tiled=True)  9.11 us
    all_to_all x1, starting transfers between devices, body(): lax.all_to_all(mine, 'expert', split_axis=0, concat_axis=0, tiled=True)  7.86 us
  transfers between devices with their start and end apart: 6, of which 5 were waited for; matrix products, arithmetic and copies ran while one was open for 4% of the time, Pallas kernels for 15%

profile of v1, /device:TPU:11, one launch (start us, length us, event | category | flops | bytes accessed | tf_op | source)
XLA Modules:
  0.0 257.7 jit_solution(2988738038637244268)
XLA Ops:
  0.0 31.2 %adapter_cut.1 = bf16[16,6,3840]{2,1,0:T(8,128)(2,1)} custom-call(s32[1]{0:T(128)} %bitcast.10.dp_ref, bf16[6,466944]{1,0:T(8,128)(2,1)} %rows.1), custom_call_target="tpu_custom_call" | custom-call | tf_op jit(solution)/shard_map/adapter_cut/pallas_call | solution.py:58
  31.2 0.0 copy-start.8
  31.2 7.9 %all-to-all-start.3 = ((bf16[16,6,3840]{2,1,0:T(8,128)(2,1)}), bf16[16,6,3840]{2,1,0:T(8,128)(2,1)S(1)}, u32[]{:S(2)}, u32[]{:S(2)}) async-start(bf16[16,6,3840]{2,1,0:T(8,128)(2,1)} %adapter_cut.1), calls=%async_computation.3 | async-start | bytes 1966080 | tf_op jit(solution)/shard_map/all_to_all | solution.py:355
  39.1 0.0 copy-done.5
  39.1 0.1 copy.34.ids
  39.2 0.0 copy-done.7
  39.2 0.2 fusion
  39.3 0.2 fusion.1
  39.5 0.0 copy-done.1
  39.6 1.8 token_dispatch.4
  41.3 10.9 %all-to-all-done.3.pieces = bf16[16,6,3840]{2,1,0:T(8,128)(2,1)S(1)} async-done(((bf16[16,6,3840]{2,1,0:T(8,128)(2,1)}), bf16[16,6,3840]{2,1,0:T(8,128)(2,1)S(1)}, u32[]{:S(2)}, u32[]{:S(2)}) %all-to-all-start.3) | async-done | bytes 737312 | tf_op jit(solution)/shard_map/all_to_all | solution.py:355
  52.3 9.9 %all-to-all-start.2 = ((bf16[128,2,2048]{2,1,0:T(2,128)(2,1)}), bf16[128,2,2048]{2,1,0:T(2,128)(2,1)S(1)}, u32[]{:S(2)}, u32[]{:S(2)}) async-start(bf16[128,2,2048]{2,1,0:T(2,128)(2,1)} %token_dispatch.4), calls=%async_computation.2 | async-start | bytes 2097152 | tf_op jit(solution)/shard_map/all_to_all | solution.py:373
  62.1 0.1 eq.47
  62.2 0.2 convert_reduce_fusion
  62.4 0.6 broadcast_compare_fusion
  63.7 0.0 copy-done.8
  63.7 0.1 select_reduce_fusion
  63.8 1.8 adapter_pick.1
  65.6 12.2 %all-to-all-done.2.x_ref = bf16[128,2,2048]{2,1,0:T(2,128)(2,1)S(1)} async-done(((bf16[128,2,2048]{2,1,0:T(2,128)(2,1)}), bf16[128,2,2048]{2,1,0:T(2,128)(2,1)S(1)}, u32[]{:S(2)}, u32[]{:S(2)}) %all-to-all-start.2) | async-done | bytes 1048608 | tf_op jit(solution)/shard_map/all_to_all | solution.py:373
  77.8 9.1 %all-to-all-start.4 = ((bf16[128,32,128]{2,1,0:T(8,128)(2,1)}), bf16[128,32,128]{2,1,0:T(8,128)(2,1)}, u32[]{:S(2)}, u32[]{:S(2)}) async-start(bf16[128,32,128]{2,1,0:T(8,128)(2,1)} %adapter_pick.1), calls=%async_computation.4 | async-start | bytes 2097152 | tf_op jit(solution)/shard_map/all_to_all | solution.py:365
  87.0 0.1 select_select_fusion
  87.1 0.1 select_n.80
  87.2 0.1 select_n.83
  87.3 0.1 broadcast_in_dim.99
  87.4 0.1 stack_reshape.2
  87.5 3.1 %token_dispatch.5 = bf16[128,4,4096]{2,1,0:T(4,128)(2,1)S(1)} custom-call(s32[64,8]{1,0:T(8,128)S(1)} %copy.34.ids, s32[2,512]{1,0:T(2,128)S(1)} %get-tuple-element.70.info, bf16[64,4096]{1,0:T(8,128)(2,1)S(1)} %copy-done.1), custom_call_target="tpu_custom_call" | custom-call | flops 268435456 | bytes 4194304 | tf_op jit(solution)/shard_map/token_dispatch/pallas_call | solution.py:134
  90.6 0.0 copy-start
  90.6 1.9 copy-done
  92.5 9.8 %all-to-all-done.4 = bf16[128,32,128]{2,1,0:T(8,128)(2,1)} async-done(((bf16[128,32,128]{2,1,0:T(8,128)(2,1)}), bf16[128,32,128]{2,1,0:T(8,128)(2,1)}, u32[]{:S(2)}, u32[]{:S(2)}) %all-to-all-start.4) | async-done | bytes 1048608 | tf_op jit(solution)/shard_map/all_to_all | solution.py:365
  102.3 0.0 copy-done.2
  102.3 9.2 %all-to-all-start.6 = ((bf16[128,4,4096]{2,1,0:T(4,128)(2,1)}), bf16[128,4,4096]{2,1,0:T(4,128)(2,1)}, u32[]{:S(2)}, u32[]{:S(2)}) async-start(bf16[128,4,4096]{2,1,0:T(4,128)(2,1)} %copy-done), calls=%async_computation.6 | async-start | bytes 8388608 | tf_op jit(solution)/shard_map/all_to_all | solution.py:373
  111.5 1.2 slice.12
  112.7 0.3 reshape.213.wide
  113.0 0.9 slice.13
  114.0 0.0 copy-start.3
  114.0 12.7 %slot_expert.4 = bf16[128,4096]{1,0:T(8,128)(2,1)} custom-call(bf16[128,2,2048]{2,1,0:T(2,128)(2,1)} %copy-done.2, bf16[4096,768]{1,0:T(8,128)(2,1)} %bitcast.20, bf16[4096,768]{1,0:T(8,128)(2,1)} %bitcast.23, bf16[768,4096]{1,0:T(8,128)(2,1)} %bitcast.26, bf16[96,4096]{1,0:T(8,128)(2,1)S(1)} %reshape.213.wide, bf16[96,768]{1,0:T(8,128)(2,1)S(1)} %bitcast.31), custom_call_target="tpu_custom_call" | custom-call | flops 2415919104 | bytes 20971520 | tf_op jit(solution)/shard_map/slot_expert/pallas_call | solution.py:232
  126.7 2.6 %reshape.215 = bf16[128,2,2048]{2,1,0:T(2,128)(2,1)} reshape(bf16[128,4096]{1,0:T(8,128)(2,1)} %slot_expert.4) | data formatting | bytes 2097152 | tf_op jit(solution)/shard_map/reshape | solution.py:383
  129.3 32.6 %all-to-all-done.6.x_ref = bf16[128,4,4096]{2,1,0:T(4,128)(2,1)} async-done(((bf16[128,4,4096]{2,1,0:T(4,128)(2,1)}), bf16[128,4,4096]{2,1,0:T(4,128)(2,1)}, u32[]{:S(2)}, u32[]{:S(2)}) %all-to-all-start.6) | async-done | bytes 4194336 | tf_op jit(solution)/shard_map/all_to_all | solution.py:373
  161.9 7.0 %all-to-all-start.5 = ((bf16[128,2,2048]{2,1,0:T(2,128)(2,1)}), bf16[128,2,2048]{2,1,0:T(2,128)(2,1)S(1)}, u32[]{:S(2)}, u32[]{:S(2)}) async-start(bf16[128,2,2048]{2,1,0:T(2,128)(2,1)} %reshape.215), calls=%async_computation.5 | async-start | bytes 2097152 | tf_op jit(solution)/shard_map/all_to_all | solution.py:373
  169.0 20.7 %slot_expert.5 = bf16[128,4,4096]{2,1,0:T(4,128)(2,1)} custom-call(bf16[128,4,4096]{2,1,0:T(4,128)(2,1)} %all-to-all-done.6.x_ref, bf16[4096,768]{1,0:T(8,128)(2,1)} %bitcast.21, bf16[4096,768]{1,0:T(8,128)(2,1)} %bitcast.24, bf16[768,4096]{1,0:T(8,128)(2,1)} %bitcast.27, bf16[96,4096]{1,0:T(8,128)(2,1)S(1)} %reshape.213.wide, bf16[96,768]{1,0:T(8,128)(2,1)S(1)} %bitcast.32), custom_call_target="tpu_custom_call" | custom-call | flops 9663676416 | bytes 27262976 | tf_op jit(solution)/shard_map/slot_expert/pallas_call | solution.py:232
  189.7 0.0 all-to-all-done.5
  189.7 10.2 %all-to-all-start.7 = ((bf16[128,4,4096]{2,1,0:T(4,128)(2,1)}), bf16[128,4,4096]{2,1,0:T(4,128)(2,1)}, u32[]{:S(2)}, u32[]{:S(2)}) async-start(bf16[128,4,4096]{2,1,0:T(4,128)(2,1)} %slot_expert.5), calls=%async_computation.7 | async-start | bytes 8388608 | tf_op jit(solution)/shard_map/all_to_all | solution.py:373
  199.9 0.1 copy.35.weight
  200.0 1.7 slice_reduce_fusion
  202.3 0.4 copy.37
  202.7 47.6 %all-to-all-done.7.answers = bf16[128,4,4096]{2,1,0:T(4,128)(2,1)} async-done(((bf16[128,4,4096]{2,1,0:T(4,128)(2,1)}), bf16[128,4,4096]{2,1,0:T(4,128)(2,1)}, u32[]{:S(2)}, u32[]{:S(2)}) %all-to-all-start.7) | async-done | bytes 4194336 | tf_op jit(solution)/shard_map/all_to_all | solution.py:373
  250.3 4.5 %token_combine.4 = f32[64,4096]{1,0:T(8,128)S(1)} custom-call(s32[64,8]{1,0:T(8,128)S(1)} %copy.34.ids, f32[64,8]{1,0:T(8,128)S(1)} %copy.35.weight, s32[2,512]{1,0:T(2,128)S(1)} %get-tuple-element.70.info, bf16[128,4,4096]{2,1,0:T(4,128)(2,1)} %all-to-all-done.7.answers), custom_call_target="tpu_custom_call" | custom-call | flops 536870912 | bytes 4194304 | tf_op jit(solution)/shard_map/token_combine/pallas_call | solution.py:293
  254.8 3.0 %token_combine.5 = bf16[64,4096]{1,0:T(8,128)(2,1)} custom-call(s32[64,8]{1,0:T(8,128)S(1)} %copy.34.ids, f32[64,8]{1,0:T(8,128)S(1)} %copy.35.weight, s32[2,128]{1,0:T(2,128)S(1)} %pad_add_fusion.2.info, bf16[128,4096]{1,0:T(8,128)(2,1)S(1)} %bitcast.18, f32[64,4096]{1,0:T(8,128)S(1)} %get-tuple-element.79.rest_0_), custom_call_target="tpu_custom_call" | custom-call | flops 134217728 | bytes 1048576 | tf_op jit(solution)/shard_map/token_combine/pallas_call | solution.py:293
  (16 shorter events, 0.1 us)
Async XLA Ops:
  0.0 39.1 %copy-start.5 = (s32[64,8]{0,1:T(8,128)S(1)}, s32[64,8]{0,1:T(8,128)}, u32[]{:S(2)}) copy-start(s32[64,8]{0,1:T(8,128)} %param.12) | copy-start | bytes 6148
  0.0 39.2 %copy-start.7 = (s32[128]{0:T(128)S(1)}, s32[128]{0:T(128)}, u32[]{:S(2)}) copy-start(s32[128]{0:T(128)} %param.14) | copy-start | bytes 1540
  0.0 39.5 %copy-start.1 = (bf16[64,4096]{1,0:T(8,128)(2,1)S(1)}, bf16[64,4096]{1,0:T(8,128)(2,1)}, u32[]{:S(2)}) copy-start(bf16[64,4096]{1,0:T(8,128)(2,1)} %tokens.3) | copy-start | bytes 1572868
  31.2 32.5 %copy-start.8 = (s32[96]{0:T(128)S(1)}, s32[96]{0:T(128)}, u32[]{:S(2)}) copy-start(s32[96]{0:T(128)} %param.18) | copy-start | bytes 1156
  31.2 21.1 %all-to-all-start.3 = ((bf16[16,6,3840]{2,1,0:T(8,128)(2,1)}), bf16[16,6,3840]{2,1,0:T(8,128)(2,1)S(1)}, u32[]{:S(2)}, u32[]{:S(2)}) async-start(bf16[16,6,3840]{2,1,0:T(8,128)(2,1)} %adapter_cut.1), calls=%async_computation.3 | async-start | bytes 1966080 | tf_op jit(solution)/shard_map/all_to_all | solution.py:355
  52.3 25.5 %all-to-all-start.2 = ((bf16[128,2,2048]{2,1,0:T(2,128)(2,1)}), bf16[128,2,2048]{2,1,0:T(2,128)(2,1)S(1)}, u32[]{:S(2)}, u32[]{:S(2)}) async-start(bf16[128,2,2048]{2,1,0:T(2,128)(2,1)} %token_dispatch.4), calls=%async_computation.2 | async-start | bytes 2097152 | tf_op jit(solution)/shard_map/all_to_all | solution.py:373
  77.8 24.5 %copy-start.2 = (bf16[128,2,2048]{2,1,0:T(2,128)(2,1)}, bf16[128,2,2048]{2,1,0:T(2,128)(2,1)S(1)}, u32[]{:S(2)}) copy-start(bf16[128,2,2048]{2,1,0:T(2,128)(2,1)S(1)} %all-to-all-done.2.x_ref) | copy-start | bytes 3145732
  77.8 24.5 %all-to-all-start.4 = ((bf16[128,32,128]{2,1,0:T(8,128)(2,1)}), bf16[128,32,128]{2,1,0:T(8,128)(2,1)}, u32[]{:S(2)}, u32[]{:S(2)}) async-start(bf16[128,32,128]{2,1,0:T(8,128)(2,1)} %adapter_pick.1), calls=%async_computation.4 | async-start | bytes 2097152 | tf_op jit(solution)/shard_map/all_to_all | solution.py:365
  90.6 2.0 copy-start
  102.3 59.6 %all-to-all-start.6 = ((bf16[128,4,4096]{2,1,0:T(4,128)(2,1)}), bf16[128,4,4096]{2,1,0:T(4,128)(2,1)}, u32[]{:S(2)}, u32[]{:S(2)}) async-start(bf16[128,4,4096]{2,1,0:T(4,128)(2,1)} %copy-done), calls=%async_computation.6 | async-start | bytes 8388608 | tf_op jit(solution)/shard_map/all_to_all | solution.py:373
  114.0 55.0 %copy-start.3 = (bf16[12,8,6,128]{3,1,2,0:T(8,128)(2,1)}, bf16[12,8,6,128]{3,1,2,0:T(8,128)(2,1)S(1)}, u32[]{:S(2)}) copy-start(bf16[12,8,6,128]{3,1,2,0:T(8,128)(2,1)S(1)} %copy.39) | copy-start | bytes 442372
  161.9 27.7 %all-to-all-start.5 = ((bf16[128,2,2048]{2,1,0:T(2,128)(2,1)}), bf16[128,2,2048]{2,1,0:T(2,128)(2,1)S(1)}, u32[]{:S(2)}, u32[]{:S(2)}) async-start(bf16[128,2,2048]{2,1,0:T(2,128)(2,1)} %reshape.215), calls=%async_computation.5 | async-start | bytes 2097152 | tf_op jit(solution)/shard_map/all_to_all | solution.py:373
  189.7 10.2 %copy-start.6 = (f32[64,8]{0,1:T(8,128)S(1)}, f32[64,8]{0,1:T(8,128)}, u32[]{:S(2)}) copy-start(f32[64,8]{0,1:T(8,128)} %param.13) | copy-start | bytes 6148
  189.7 60.6 %all-to-all-start.7 = ((bf16[128,4,4096]{2,1,0:T(4,128)(2,1)}), bf16[128,4,4096]{2,1,0:T(4,128)(2,1)}, u32[]{:S(2)}, u32[]{:S(2)}) async-start(bf16[128,4,4096]{2,1,0:T(4,128)(2,1)} %slot_expert.5), calls=%async_computation.7 | async-start | bytes 8388608 | tf_op jit(solution)/shard_map/all_to_all | solution.py:373

commit v2 on v1

v2 whole, which is shorter than its diff:
```python
import functools

import jax
import jax.numpy as jnp
from jax import lax
from jax.experimental import pallas as pl
from jax.experimental.pallas import tpu as pltpu
from jax.sharding import PartitionSpec as P

bf16 = jnp.bfloat16
f32 = jnp.float32
MIB = 1 << 20

PLACES = 5
MOST = 8


def params(limit_mib):
    return pltpu.CompilerParams(vmem_limit_bytes=limit_mib * MIB)


def whole(shape):
    return pl.BlockSpec(shape, lambda *_: (0,) * len(shape))


def cut_kernel(wide_rows, narrow, dp_size, limit, where, ids, serving, column, rows, out, cut, sems):
    groups, held, model = cut.shape
    dp_index = where[0]
    first_narrow = wide_rows // dp_size
    rank = wide_rows // 3
    copies = []
    for e in range(groups):
        piece = e * dp_size + dp_index
        if e < first_narrow:
            spans = [(piece * model, 0, model)]
        else:
            q = piece - wide_rows
            spans = [
                (wide_rows * model + (g * rank + q) * narrow, g * narrow, narrow) for g in range(3)
            ]
        for source, target, width in spans:
            copies.append(
                pltpu.make_async_copy(
                    rows.at[:, pl.ds(pl.multiple_of(source, 128), width)],
                    cut.at[e, :, pl.ds(target, width)],
                    sems.at[len(copies)],
                )
            )
    for copy in copies:
        copy.start()
    slots = serving.shape[1]
    named = jnp.zeros((ids.shape[0], slots), f32)
    for k in range(ids.shape[1]):
        named = named + (ids[:, k : k + 1] == serving[...]).astype(f32)
    named = jnp.sum(named, axis=0, keepdims=True)
    holders = jnp.sum((column[...] == serving[...]).astype(f32), axis=0, keepdims=True)
    over = jnp.where((named > limit) & (holders < 2.0), 1.0, 0.0)
    over = jnp.max(over, axis=1, keepdims=True)
    for e in range(first_narrow, groups):
        cut[e, :, 3 * narrow :] = jnp.broadcast_to(over, (held, model - 3 * narrow)).astype(bf16)
    for copy in copies:
        copy.wait()
    for e in range(groups):
        out[e] = cut[e].reshape(out.shape[1:])


def cut_pieces(rows, dp_index, ids, serving, limit, groups, dp_size, model, narrow, rank):
    held = rows.shape[0]
    slots = serving.shape[0]
    wide_rows = 3 * rank
    first_narrow = wide_rows // dp_size
    held_in = pl.BlockSpec(memory_space=pltpu.VMEM)
    return pl.pallas_call(
        functools.partial(cut_kernel, wide_rows, narrow, dp_size, limit),
        in_specs=[
            pl.BlockSpec(memory_space=pltpu.SMEM),
            held_in,
            held_in,
            held_in,
            pl.BlockSpec(memory_space=pltpu.HBM),
        ],
        out_specs=held_in,
        out_shape=jax.ShapeDtypeStruct((groups, held * model // 128, 128), bf16),
        scratch_shapes=[
            pltpu.VMEM((groups, held, model), bf16),
            pltpu.SemaphoreType.DMA((first_narrow + 3 * (groups - first_narrow),)),
        ],
        compiler_params=params(16),
        name="adapter_cut",
    )(dp_index.reshape(1), ids, serving.reshape(1, slots), serving.reshape(slots, 1), rows)


def pick_kernel(held, flag_at, where, wanted, pieces, cells, out, rows):
    groups = pieces.shape[0]
    model = rows.shape[1]
    slots = out.shape[0]
    rows[...] = jnp.zeros_like(rows)
    for e in range(groups):
        rows[8 * e : 8 * e + held, :] = pieces[e].reshape(held, model).astype(f32)
    want = wanted[...]
    place = (want // held) * 8 + want % held
    chosen = lax.broadcasted_iota(jnp.int32, (8 * groups, slots), 0) == place
    picked = lax.dot_general(
        chosen.astype(bf16),
        rows[...].astype(bf16),
        (((0,), (0,)), ((), ())),
        preferred_element_type=f32,
    )
    flags = jnp.max(rows[:, flag_at : flag_at + 128], axis=0, keepdims=True)
    kept = picked[:, flag_at : flag_at + 128]
    flags = jnp.where(where[0] > 0, jnp.broadcast_to(flags, kept.shape), kept)
    full = jnp.concatenate([picked[:, :flag_at], flags, picked[:, flag_at + 128 :]], axis=1)
    out[...] = full.astype(bf16).reshape(out.shape)


def pick_pieces(pieces, held, wanted, holds_flag, flag_at, cells):
    groups = pieces.shape[0]
    model = pieces.shape[1] * pieces.shape[2] // held
    slots, units, lanes = cells.shape
    block = (slots, model // lanes, lanes)
    last = units * lanes // model - 1
    return pl.pallas_call(
        functools.partial(pick_kernel, held, flag_at),
        grid=(1,),
        in_specs=[
            pl.BlockSpec(memory_space=pltpu.SMEM),
            whole((1, slots)),
            whole(pieces.shape),
            pl.BlockSpec(memory_space=pl.ANY),
        ],
        out_specs=pl.BlockSpec(block, lambda i: (0, last, 0)),
        out_shape=jax.ShapeDtypeStruct(cells.shape, bf16),
        input_output_aliases={3: 0},
        scratch_shapes=[pltpu.VMEM((8 * groups, model), f32)],
        compiler_params=params(24),
        name="adapter_pick",
    )(holds_flag.reshape(1), wanted.reshape(1, slots), pieces, cells)


def placement(ids, info):
    tokens = ids.shape[0]
    named = ids[:, 0:1] == info[0:1, :]
    for k in range(1, ids.shape[1]):
        named = named | (ids[:, k : k + 1] == info[0:1, :])
    before = lax.broadcasted_iota(jnp.int32, (tokens, tokens), 0) > lax.broadcasted_iota(
        jnp.int32, (tokens, tokens), 1
    )
    rank = jnp.dot(before.astype(bf16), named.astype(bf16), preferred_element_type=f32)
    return named & (rank == info[1:2, :].astype(f32))


def dispatch_kernel(ids, info, tokens, out):
    fills = placement(ids[...], info[0]).astype(bf16)
    sent = lax.dot_general(
        fills, tokens[...], (((0,), (0,)), ((), ())), preferred_element_type=f32
    )
    out[...] = sent.astype(bf16).reshape(out.shape)


def dispatch(ids, info, tokens):
    places, _, slots = info.shape
    count, model = tokens.shape
    return pl.pallas_call(
        dispatch_kernel,
        grid=(places,),
        in_specs=[
            whole(ids.shape),
            pl.BlockSpec((1, 2, slots), lambda j: (j, 0, 0)),
            whole(tokens.shape),
        ],
        out_specs=pl.BlockSpec((slots, model // 128, 128), lambda j: (0, j, 0)),
        out_shape=jax.ShapeDtypeStruct((slots, (places + 1) * model // 128, 128), bf16),
        compiler_params=params(24),
        cost_estimate=pl.CostEstimate(
            flops=2 * places * slots * count * model,
            bytes_accessed=2 * places * slots * model,
            transcendentals=0,
        ),
        name="token_dispatch",
    )(ids, info, tokens)


def expert_kernel(
    rank,
    cells,
    gate_hbm,
    up_hbm,
    down_hbm,
    out,
    gate,
    up,
    down,
    x,
    factors,
    shrunk,
    hidden,
    sent,
    gate_sems,
    up_sems,
    down_sems,
    out_sems,
):
    slots = cells.shape[0]
    rows, model = x.shape
    units = hidden.shape[1]
    row = model // 128
    places = rows // slots
    tile = units // gate_sems.shape[0]
    width = sent.shape[2] * 128
    up_tiles, down_tiles = units // tile, model // width

    def tile_at(i, size):
        return pl.ds(pl.multiple_of(i * size, size), size)

    def load(i, source, target, size, sems):
        at = tile_at(i, size)
        return pltpu.make_async_copy(source.at[:, at], target.at[:, at], sems.at[i])

    def load_gate(i):
        return load(i, gate_hbm, gate, tile, gate_sems)

    def load_up(i):
        return load(i, up_hbm, up, tile, up_sems)

    def load_down(i):
        return load(i, down_hbm, down, width, down_sems)

    def send(i, j):
        at = pl.ds(pl.multiple_of(j * row + i * (width // 128), 8), width // 128)
        return pltpu.make_async_copy(sent.at[j], out.at[:, at, :], out_sems.at[i * places + j])

    for i in range(up_tiles):
        load_gate(i).start()
        load_up(i).start()
    for i in range(down_tiles):
        load_down(i).start()

    factors[...] = cells[:, places * row :, :].reshape(slots, model)

    @pl.loop(0, places)
    def _(j):
        here = tile_at(j, slots)
        part = cells[:, tile_at(j, row), :].reshape(slots, model)
        x[here, :] = part
        shrunk[here, :] = lax.dot_general(
            part,
            factors[0 : 2 * rank, :],
            (((1,), (1,)), ((), ())),
            preferred_element_type=f32,
        ).astype(bf16)

    @pl.loop(0, up_tiles)
    def _(i):
        at = tile_at(i, tile)
        load_gate(i).wait()
        load_up(i).wait()
        into_gate = jnp.dot(x[...], gate[:, at], preferred_element_type=f32) + jnp.dot(
            shrunk[:, :rank], factors[3 * rank : 4 * rank, at], preferred_element_type=f32
        )
        up_at = pl.ds(pl.multiple_of(units + i * tile, tile), tile)
        into_up = jnp.dot(x[...], up[:, at], preferred_element_type=f32) + jnp.dot(
            shrunk[:, rank:], factors[3 * rank : 4 * rank, up_at], preferred_element_type=f32
        )
        hidden[:, at] = (into_gate / (1.0 + jnp.exp(-into_gate)) * into_up).astype(bf16)

    shrunk_down = lax.dot_general(
        hidden[...],
        factors[3 * rank : 4 * rank, 2 * units : 3 * units],
        (((1,), (1,)), ((), ())),
        preferred_element_type=f32,
    ).astype(bf16)

    @pl.loop(0, down_tiles)
    def _(i):
        at = tile_at(i, width)
        load_down(i).wait()
        total = jnp.dot(hidden[...], down[:, at], preferred_element_type=f32) + jnp.dot(
            shrunk_down, factors[2 * rank : 3 * rank, at], preferred_element_type=f32
        )
        for j in range(places):

            @pl.when(i > 0)
            def _():
                send(i - 1, j).wait()

            part = total[j * slots : (j + 1) * slots].astype(bf16)
            sent[j] = part.reshape(slots, width // 128, 128)
            send(i, j).start()

    for j in range(places):
        send(down_tiles - 1, j).wait()


def expert(cells, gate, up, down, rank):
    model, units = gate.shape
    slots = cells.shape[0]
    places = cells.size // model // slots - 1
    rows = slots * places
    tile, width = 256, 1024
    in_hbm = pl.BlockSpec(memory_space=pltpu.HBM)
    return pl.pallas_call(
        functools.partial(expert_kernel, rank),
        in_specs=[pl.BlockSpec(memory_space=pltpu.VMEM)] + [in_hbm] * 3,
        out_specs=in_hbm,
        out_shape=jax.ShapeDtypeStruct((slots, places * model // 128, 128), bf16),
        scratch_shapes=[
            pltpu.VMEM((model, units), bf16),
            pltpu.VMEM((model, units), bf16),
            pltpu.VMEM((units, model), bf16),
            pltpu.VMEM((rows, model), bf16),
            pltpu.VMEM((slots, model), bf16),
            pltpu.VMEM((rows, 2 * rank), bf16),
            pltpu.VMEM((rows, units), bf16),
            pltpu.VMEM((places, slots, width // 128, 128), bf16),
            pltpu.SemaphoreType.DMA((units // tile,)),
            pltpu.SemaphoreType.DMA((units // tile,)),
            pltpu.SemaphoreType.DMA((model // width,)),
            pltpu.SemaphoreType.DMA((places * (model // width),)),
        ],
        compiler_params=params(48),
        cost_estimate=pl.CostEstimate(
            flops=6 * rows * model * units,
            bytes_accessed=6 * model * units + 4 * rows * model,
            transcendentals=rows * units,
        ),
        name="slot_expert",
    )(cells, gate, up, down)


def combine_kernel(ids, weight, info, answers, *rest):
    block, out = rest[-1], rest[-2]
    count, model = out.shape
    rows, width = block.shape
    slots = answers.shape[0]
    places = rows // slots
    row = model // 128
    fills = placement(ids[...], info[...])
    given = jnp.zeros(fills.shape, f32)
    for k in range(ids.shape[1]):
        given = given + jnp.where(ids[:, k : k + 1] == info[0:1, :], weight[:, k : k + 1], 0.0)
    given = jnp.where(fills, given, 0.0)
    high = given.astype(bf16)
    low = (given - high.astype(f32)).astype(bf16)
    both = jnp.concatenate([high, low], axis=0)

    @pl.loop(0, model // width)
    def _(i):
        at = pl.ds(pl.multiple_of(i * width, width), width)
        for j in range(places):
            units = pl.ds(pl.multiple_of(j * row + i * (width // 128), 8), width // 128)
            block[j * slots : (j + 1) * slots, :] = answers[:, units, :].reshape(slots, width)
        total = jnp.dot(both, block[...], preferred_element_type=f32)
        total = total[:count] + total[count:]
        if len(rest) == 3:
            total = total + rest[0][:, at]
        out[:, at] = total.astype(out.dtype)


def combine(ids, weight, info, answers, before=None, kind=f32):
    count = ids.shape[0]
    places, _, slots = info.shape
    model = answers.size // places // slots
    held = pl.BlockSpec(memory_space=pltpu.VMEM)
    more = () if before is None else (before,)
    info = info.transpose(1, 0, 2).reshape(2, places * slots)
    return pl.pallas_call(
        combine_kernel,
        in_specs=[held] * (4 + len(more)),
        out_specs=held,
        out_shape=jax.ShapeDtypeStruct((count, model), kind),
        scratch_shapes=[pltpu.VMEM((places * slots, 1024), bf16)],
        compiler_params=params(24),
        cost_estimate=pl.CostEstimate(
            flops=4 * count * places * slots * model,
            bytes_accessed=2 * places * slots * model,
            transcendentals=0,
        ),
        name="token_combine",
    )(ids, weight, info, answers, *more)


def body(
    tokens,
    ids,
    weight,
    serving,
    gate,
    up,
    down,
    trainer_order,
    trainer_rows,
):
    groups = lax.axis_size("expert")
    dp_size = lax.axis_size("dp")
    dp_index = lax.axis_index("dp").astype(jnp.int32)
    slots = serving.shape[0]
    experts = trainer_order.shape[0]
    held, packed = trainer_rows.shape
    count, model = tokens.shape
    units = gate.shape[2]
    rank = packed // (3 * (model + units))
    everyone = ("expert", "dp")

    slot_at = jnp.arange(slots, dtype=jnp.int32)
    same = serving[:, None] == serving[None, :]
    second = jnp.any(same & (slot_at[None, :] < slot_at[:, None]), axis=1)
    hot = jnp.sum(same.astype(jnp.int32), axis=1) > 1

    def places_info(first, last):
        at = jnp.arange(first, last, dtype=jnp.int32)[:, None]
        ranks = jnp.where(hot[None, :], 2 * at + second[None, :].astype(jnp.int32), at)
        who = jnp.broadcast_to(serving[None, :], ranks.shape)
        return jnp.stack([who, ranks], axis=1)

    mine = cut_pieces(
        trainer_rows, dp_index, ids, serving, PLACES, groups, dp_size, model, units, rank
    )
    spread = lax.all_to_all(mine, "expert", split_axis=0, concat_axis=0, tiled=True)
    trainer_row = jnp.sum(
        jnp.where(
            serving[:, None] == trainer_order[None, :],
            jnp.arange(experts, dtype=jnp.int32)[None, :],
            0,
        ),
        axis=1,
    )
    holds_flag = (lax.axis_index("expert") * dp_size + dp_index >= 3 * rank).astype(jnp.int32)

    def there(cells):
        return lax.all_to_all(cells, everyone, split_axis=0, concat_axis=0, tiled=True)

    def run(info):
        cells = dispatch(ids, info, tokens)
        cells = there(pick_pieces(spread, held, trainer_row, holds_flag, 3 * units, cells))
        return cells, there(expert(cells, gate[0], up[0], down[0], rank))

    info = places_info(0, PLACES)
    cells, answers = run(info)
    flags = cells[3 * rank :, (PLACES * model + 3 * units) // 128, 0]

    def one_round():
        return combine(ids, weight, info, answers, None, bf16)

    def two_rounds():
        more = places_info(PLACES, MOST)
        return combine(ids, weight, more, run(more)[1], combine(ids, weight, info, answers), bf16)

    return lax.cond(jnp.max(flags.astype(f32)) > 0.0, two_rounds, one_round)


def solution(mesh):
    split = P(("expert", "dp"), None)
    slot = P(("expert", "dp"), None, None)
    placed = (split, split, split, P(), slot, slot, slot, P(), P("expert", None))
    return jax.shard_map(body, mesh=mesh, in_specs=placed, out_specs=split, check_vma=False)
```

time: 262 us -> 219 us (0.84); the launches traced: 258 us -> 218 us
  blocking collectives: 0 us -> 82.3 us
  waiting for transfers between devices: 113 us -> 64.6 us
  Pallas kernels: 78.5 us -> 39.5 us
  starting transfers between devices: 53.3 us -> 16.1 us
  local copies, waits for them, and re-layouts: 8.15 us -> 12.6 us
    all_to_all x0 -> x1, blocking collectives: none -> 82.3 us  [there(): lax.all_to_all(cells, everyone, split_axis=0, concat_axis=0, tiled=True)]
    pallas_call x8 -> x5, Pallas kernels: 78.5 us -> 39.5 us  [the longest x1 23.4 us: expert(): pl.pallas_call(functools.partial(expert_kernel, rank), in_specs=[pl.Block...]
    all_to_all x4 -> x1, waiting for transfers between devices: 92.4 us -> 61.5 us  [there(): lax.all_to_all(cells, everyone, split_axis=0, concat_axis=0, tiled=True)]
    all_to_all x4 -> x1, starting transfers between devices: 36.3 us -> 8.24 us  [there(): lax.all_to_all(cells, everyone, split_axis=0, concat_axis=0, tiled=True)]
    all_to_all x1 -> x0, waiting for transfers between devices: 9.76 us -> none  [body(): lax.all_to_all(picked, everyone, split_axis=0, concat_axis=0, tiled=True)]
    unnamed x20 -> x19, local copies, waits for them, and re-layouts: 2.54 us -> 11.6 us
    all_to_all x1 -> x0, starting transfers between devices: 9.11 us -> none  [body(): lax.all_to_all(picked, everyone, split_axis=0, concat_axis=0, tiled=True)]
    all_to_all x1, waiting for transfers between devices: 10.9 us -> 3.1 us  [body(): lax.all_to_all(mine, 'expert', split_axis=0, concat_axis=0, tiled=True)]
  transfers between devices with their start and end apart: 6 -> 2, of which waited for: 5 -> 2; matrix products, arithmetic and copies ran while one was open for 4% -> 1% of each run, Pallas kernels for 15% -> 2%
where the time goes in v2:
time: 219 us; the launch traced here: 218 us
  blocking collectives  82.3 us (38%)
  waiting for transfers between devices  64.6 us (29%)
  Pallas kernels  39.5 us (18%)
  starting transfers between devices  16.1 us (7%)
  local copies, waits for them, and re-layouts  12.6 us (6%)
    all_to_all x1, blocking collectives, there(): lax.all_to_all(cells, everyone, split_axis=0, concat_axis=0, tiled=True)  82.3 us
    all_to_all x1, waiting for transfers between devices, there(): lax.all_to_all(cells, everyone, split_axis=0, concat_axis=0, tiled=True)  61.5 us
    pallas_call x1, Pallas kernels, expert(): pl.pallas_call(functools.partial(expert_kernel, rank), in_specs=[pl.Block...  23.4 us
    unnamed x19, local copies, waits for them, and re-layouts  11.6 us
    all_to_all x1, starting transfers between devices, there(): lax.all_to_all(cells, everyone, split_axis=0, concat_axis=0, tiled=True)  8.24 us
    all_to_all x1, starting transfers between devices, body(): lax.all_to_all(mine, 'expert', split_axis=0, concat_axis=0, tiled=True)  7.86 us
    pallas_call x1, Pallas kernels, combine(): pl.pallas_call(combine_kernel, in_specs=[held] * (4 + len(more)), out_spe...  6.45 us
    pallas_call x1, Pallas kernels, dispatch(): pl.pallas_call(dispatch_kernel, grid=(places,), in_specs=[whole(ids.shape...  4.84 us
  transfers between devices with their start and end apart: 2, of which 2 were waited for; matrix products, arithmetic and copies ran while one was open for 1% of the time, Pallas kernels for 2%

profile of v2, /device:TPU:11, one launch (start us, length us, event | category | flops | bytes accessed | tf_op | source)
XLA Modules:
  0.0 217.8 jit_solution(3583500477127430313)
XLA Ops:
  0.0 0.0 copy-start.10
  0.0 0.8 copy.32.ids
  0.8 0.8 copy.33.column
  1.5 0.0 copy-start.2
  1.6 3.1 %copy-done.2 = bf16[6,466944]{1,0:T(8,128)(2,1)S(1)} copy-done((bf16[6,466944]{1,0:T(8,128)(2,1)S(1)}, bf16[6,466944]{1,0:T(8,128)(2,1)}, u32[]{:S(2)}) %copy-start.2) | copy-done | bytes 5603352
  4.7 0.0 copy-start.7
  4.7 3.5 %adapter_cut.1 = bf16[16,192,128]{2,1,0:T(8,128)(2,1)} custom-call(s32[1]{0:T(128)} %bitcast.12.where, s32[64,8]{1,0:T(8,128)S(1)} %copy.32.ids, s32[1,128]{1,0:T(1,128)} %bitcast.36, s32[128,1]{1,0:T(8,128)S(1)} %copy.33.column, bf16[6,466944]{1,0:T(8,128)(2,1)S(1)} %copy-done.2), custom_call_target="tpu_custom_call" | custom-call | tf_op jit(solution)/shard_map/adapter_cut/pallas_call | solution.py:73
  8.2 0.0 copy-start.12
  8.2 7.9 %all-to-all-start.2 = ((bf16[16,192,128]{2,1,0:T(8,128)(2,1)}), bf16[16,192,128]{2,1,0:T(8,128)(2,1)S(1)}, u32[]{:S(2)}, u32[]{:S(2)}) async-start(bf16[16,192,128]{2,1,0:T(8,128)(2,1)} %adapter_cut.1), calls=%async_computation.2 | async-start | bytes 1572864 | tf_op jit(solution)/shard_map/all_to_all | solution.py:418
  16.1 0.0 copy-done.10
  16.1 0.2 fusion.1
  16.2 0.2 fusion.2
  16.5 0.1 broadcast_select_fusion.1
  16.6 0.0 copy-done.7
  16.6 4.8 %token_dispatch.3.cells = bf16[128,192,128]{2,1,0:T(8,128)(2,1)S(1)} custom-call(s32[64,8]{1,0:T(8,128)S(1)} %copy.32.ids, s32[5,2,128]{2,1,0:T(2,128)S(1)} %pad_add_fusion.1.info, bf16[64,4096]{1,0:T(8,128)(2,1)S(1)} %copy-done.7), custom_call_target="tpu_custom_call" | custom-call | flops 335544320 | bytes 5242880 | tf_op jit(solution)/shard_map/token_dispatch/pallas_call | solution.py:163
  21.4 0.0 copy-start
  21.4 2.7 %copy-done = bf16[128,192,128]{2,1,0:T(8,128)(2,1)} copy-done((bf16[128,192,128]{2,1,0:T(8,128)(2,1)}, bf16[128,192,128]{2,1,0:T(8,128)(2,1)S(1)}, u32[]{:S(2)}) %copy-start) | copy-done | bytes 6291480
  24.1 0.0 copy-done.12
  24.1 0.1 select_reduce_fusion
  24.2 3.1 %all-to-all-done.2.pieces = bf16[16,192,128]{2,1,0:T(8,128)(2,1)S(1)} async-done(((bf16[16,192,128]{2,1,0:T(8,128)(2,1)}), bf16[16,192,128]{2,1,0:T(8,128)(2,1)S(1)}, u32[]{:S(2)}, u32[]{:S(2)}) %all-to-all-start.2) | async-done | bytes 786464 | tf_op jit(solution)/shard_map/all_to_all | solution.py:418
  27.3 0.0 copy-start.1
  27.3 2.8 %copy-done.1 = bf16[128,192,128]{2,1,0:T(8,128)(2,1)S(1)} copy-done((bf16[128,192,128]{2,1,0:T(8,128)(2,1)S(1)}, bf16[128,192,128]{2,1,0:T(8,128)(2,1)}, u32[]{:S(2)}) %copy-start.1) | copy-done | bytes 6291480
  30.1 1.2 adapter_pick.3
  31.3 82.3 %all_to_all.24.cells = bf16[128,192,128]{2,1,0:T(8,128)(2,1)} all-to-all(bf16[128,192,128]{2,1,0:T(8,128)(2,1)S(1)} %adapter_pick.3), channel_id=1, replica_groups=mesh['expert'=16,'dp'=8] {'expert','dp'}, dimensions={0} | all-to-all | bytes 12582912 | tf_op jit(solution)/shard_map/all_to_all | solution.py:430
  113.6 23.4 %slot_expert.3 = bf16[128,160,128]{2,1,0:T(8,128)(2,1)S(1)} custom-call(bf16[128,192,128]{2,1,0:T(8,128)(2,1)} %all_to_all.24.cells, bf16[4096,768]{1,0:T(8,128)(2,1)} %bitcast.39, bf16[4096,768]{1,0:T(8,128)(2,1)} %bitcast.43, bf16[768,4096]{1,0:T(8,128)(2,1)} %bitcast.45), custom_call_target="tpu_custom_call" | custom-call | flops 12079595520 | bytes 29360128 | tf_op jit(solution)/shard_map/slot_expert/pallas_call | solution.py:301
  137.0 0.0 copy-start.3
  137.0 2.3 %copy-done.3 = bf16[128,160,128]{2,1,0:T(8,128)(2,1)} copy-done((bf16[128,160,128]{2,1,0:T(8,128)(2,1)}, bf16[128,160,128]{2,1,0:T(8,128)(2,1)S(1)}, u32[]{:S(2)}) %copy-start.3) | copy-done | bytes 5242904
  139.3 0.0 copy-start.8
  139.3 0.0 copy-start.9
  139.3 8.2 %all-to-all-start.4 = ((bf16[128,160,128]{2,1,0:T(8,128)(2,1)}), bf16[128,160,128]{2,1,0:T(8,128)(2,1)}, u32[]{:S(2)}, u32[]{:S(2)}) async-start(bf16[128,160,128]{2,1,0:T(8,128)(2,1)} %copy-done.3), calls=%async_computation.4 | async-start | bytes 10485760 | tf_op jit(solution)/shard_map/all_to_all | solution.py:430
  147.5 1.5 slice_reduce_fusion
  149.7 61.5 %all-to-all-done.4 = bf16[128,160,128]{2,1,0:T(8,128)(2,1)} async-done(((bf16[128,160,128]{2,1,0:T(8,128)(2,1)}), bf16[128,160,128]{2,1,0:T(8,128)(2,1)}, u32[]{:S(2)}, u32[]{:S(2)}) %all-to-all-start.4) | async-done | bytes 5242912 | tf_op jit(solution)/shard_map/all_to_all | solution.py:430
  211.1 0.0 copy-done.8
  211.1 0.0 copy-done.9
  211.1 6.6 %conditional.1 = (bf16[64,4096]{1,0:T(8,128)(2,1)}) conditional(s32[]{:T(128)} %convert_element_type.25, (s32[5,2,128]{2,1,0:T(2,128)S(1)}, s32[64,8]{0,1:T(8,128)S(1)}, f32[64,8]{0,1:T(8,128)S(1)}, bf16[128,160,128]{2,1,0:T(8,128)(2,1)}) %tuple.28, (s32[128]{0:T(128)S(1)}, s32[128]{0:T(128)S(1)}, pred[128]{0:T(512)(128)(4,1)S(1)}, s32[]{:T(128)}, ...), branch_computations={%region_4.5_spmd, %region_5.6_spmd} | conditional | flops 8522827776 | bytes 119581312 | solution.py:448
  211.1 0.1 copy.36.ids
  211.2 0.1 copy.37.weight
  211.3 6.4 %token_combine.3 = bf16[64,4096]{1,0:T(8,128)(2,1)} custom-call(s32[64,8]{1,0:T(8,128)S(1)} %copy.36.ids, f32[64,8]{1,0:T(8,128)S(1)} %copy.37.weight, s32[2,640]{1,0:T(2,128)S(1)} %bitcast.31, bf16[128,160,128]{2,1,0:T(8,128)(2,1)} %get-tuple-element.50.answers), custom_call_target="tpu_custom_call" | custom-call | flops 671088640 | bytes 5242880 | tf_op jit(solution)/shard_map/cond/branch_0_fun/token_combine/pallas_call | solution.py:366
  (7 shorter events, 0.0 us)
Async XLA Ops:
  0.0 16.1 %copy-start.10 = (s32[128]{0:T(128)S(1)}, s32[128]{0:T(128)}, u32[]{:S(2)}) copy-start(s32[128]{0:T(128)} %param.14) | copy-start | bytes 1540
  1.5 3.1 %copy-start.2 = (bf16[6,466944]{1,0:T(8,128)(2,1)S(1)}, bf16[6,466944]{1,0:T(8,128)(2,1)}, u32[]{:S(2)}) copy-start(bf16[6,466944]{1,0:T(8,128)(2,1)} %rows.1) | copy-start | bytes 16809988
  4.7 11.9 %copy-start.7 = (bf16[64,4096]{1,0:T(8,128)(2,1)S(1)}, bf16[64,4096]{1,0:T(8,128)(2,1)}, u32[]{:S(2)}) copy-start(bf16[64,4096]{1,0:T(8,128)(2,1)} %tokens.1) | copy-start | bytes 1572868
  8.2 15.9 %copy-start.12 = (s32[96]{0:T(128)S(1)}, s32[96]{0:T(128)}, u32[]{:S(2)}) copy-start(s32[96]{0:T(128)} %param.18) | copy-start | bytes 1156
  8.2 19.1 %all-to-all-start.2 = ((bf16[16,192,128]{2,1,0:T(8,128)(2,1)}), bf16[16,192,128]{2,1,0:T(8,128)(2,1)S(1)}, u32[]{:S(2)}, u32[]{:S(2)}) async-start(bf16[16,192,128]{2,1,0:T(8,128)(2,1)} %adapter_cut.1), calls=%async_computation.2 | async-start | bytes 1572864 | tf_op jit(solution)/shard_map/all_to_all | solution.py:418
  21.4 2.7 %copy-start = (bf16[128,192,128]{2,1,0:T(8,128)(2,1)}, bf16[128,192,128]{2,1,0:T(8,128)(2,1)S(1)}, u32[]{:S(2)}) copy-start(bf16[128,192,128]{2,1,0:T(8,128)(2,1)S(1)} %token_dispatch.3.cells) | copy-start | bytes 18874372
  27.3 2.8 %copy-start.1 = (bf16[128,192,128]{2,1,0:T(8,128)(2,1)S(1)}, bf16[128,192,128]{2,1,0:T(8,128)(2,1)}, u32[]{:S(2)}) copy-start(bf16[128,192,128]{2,1,0:T(8,128)(2,1)} %copy-done) | copy-start | bytes 18874372
  137.0 2.3 %copy-start.3 = (bf16[128,160,128]{2,1,0:T(8,128)(2,1)}, bf16[128,160,128]{2,1,0:T(8,128)(2,1)S(1)}, u32[]{:S(2)}) copy-start(bf16[128,160,128]{2,1,0:T(8,128)(2,1)S(1)} %slot_expert.3) | copy-start | bytes 15728644
  139.3 71.9 %copy-start.8 = (s32[64,8]{0,1:T(8,128)S(1)}, s32[64,8]{0,1:T(8,128)}, u32[]{:S(2)}) copy-start(s32[64,8]{0,1:T(8,128)} %param.12) | copy-start | bytes 6148
  139.3 71.9 %copy-start.9 = (f32[64,8]{0,1:T(8,128)S(1)}, f32[64,8]{0,1:T(8,128)}, u32[]{:S(2)}) copy-start(f32[64,8]{0,1:T(8,128)} %param.13) | copy-start | bytes 6148
  139.3 71.9 %all-to-all-start.4 = ((bf16[128,160,128]{2,1,0:T(8,128)(2,1)}), bf16[128,160,128]{2,1,0:T(8,128)(2,1)}, u32[]{:S(2)}, u32[]{:S(2)}) async-start(bf16[128,160,128]{2,1,0:T(8,128)(2,1)} %copy-done.3), calls=%async_computation.4 | async-start | bytes 10485760 | tf_op jit(solution)/shard_map/all_to_all | solution.py:430

commit v3 on v2

v3 whole, which is shorter than its diff:
```python
import functools

import jax
import jax.numpy as jnp
from jax import lax
from jax.experimental import pallas as pl
from jax.experimental.pallas import tpu as pltpu
from jax.sharding import PartitionSpec as P

bf16 = jnp.bfloat16
f32 = jnp.float32
MIB = 1 << 20
ALL_MIB = 60

PLACES = 5
MOST = 8

VMEM = pl.BlockSpec(memory_space=pltpu.VMEM)
HBM = pl.BlockSpec(memory_space=pltpu.HBM)


def params(limit_mib):
    return pltpu.CompilerParams(vmem_limit_bytes=limit_mib * MIB)


def whole(shape):
    return pl.BlockSpec(shape, lambda *_: (0,) * len(shape))


def tile_at(i, size):
    return pl.ds(pl.multiple_of(i * size, size), size)


def beside(serving):
    across = jnp.broadcast_to(serving, (serving.shape[1],) * 2)
    return across.T, across


def cut_kernel(wide_rows, narrow, dp_size, limit, ids, serving, rows, out, cut, sems):
    groups, held, model = cut.shape
    dp_index = lax.axis_index("dp")
    first_narrow = wide_rows // dp_size
    rank = wide_rows // 3
    copies = []
    for e in range(groups):
        piece = e * dp_size + dp_index
        if e < first_narrow:
            spans = [(piece * model, 0, model)]
        else:
            q = piece - wide_rows
            spans = [
                (wide_rows * model + (g * rank + q) * narrow, g * narrow, narrow) for g in range(3)
            ]
        for source, target, width in spans:
            copies.append(
                pltpu.make_async_copy(
                    rows.at[:, pl.ds(pl.multiple_of(source, 128), width)],
                    cut.at[e, :, pl.ds(target, width)],
                    sems.at[len(copies)],
                )
            )
    for copy in copies:
        copy.start()
    mine, other = beside(serving[...])
    named = jnp.zeros((serving.shape[1], ids.shape[1]), f32)
    for k in range(ids.shape[0]):
        named = named + (mine[:, : ids.shape[1]] == ids[k : k + 1, :]).astype(f32)
    named = jnp.sum(named, axis=1, keepdims=True)
    holders = jnp.sum((mine == other).astype(f32), axis=1, keepdims=True)
    over = jnp.where((named > limit) & (holders < 2.0), 1.0, 0.0)
    over = jnp.max(over, axis=0, keepdims=True)
    for e in range(first_narrow, groups):
        cut[e, :, 3 * narrow :] = jnp.broadcast_to(over, (held, model - 3 * narrow)).astype(bf16)
    for copy in copies:
        copy.wait()
    for e in range(groups):
        out[e] = cut[e].reshape(out.shape[1:])


def cut_pieces(rows, ids, serving, limit, groups, dp_size, model, narrow, rank):
    held = rows.shape[0]
    wide_rows = 3 * rank
    first_narrow = wide_rows // dp_size
    return pl.pallas_call(
        functools.partial(cut_kernel, wide_rows, narrow, dp_size, limit),
        in_specs=[VMEM, VMEM, HBM],
        out_specs=VMEM,
        out_shape=jax.ShapeDtypeStruct((groups, held * model // 128, 128), bf16),
        scratch_shapes=[
            pltpu.VMEM((groups, held, model), bf16),
            pltpu.SemaphoreType.DMA((first_narrow + 3 * (groups - first_narrow),)),
        ],
        compiler_params=params(ALL_MIB),
        name="adapter_cut",
    )(ids, serving, rows)


def pick_kernel(held, flag_at, first_narrow, wanted, pieces, cells, out, rows):
    groups = pieces.shape[0]
    model = rows.shape[1]
    slots = out.shape[0]
    rows[...] = jnp.zeros_like(rows)
    for e in range(groups):
        rows[8 * e : 8 * e + held, :] = pieces[e].reshape(held, model).astype(f32)
    want = wanted[...]
    place = (want // held) * 8 + want % held
    chosen = lax.broadcasted_iota(jnp.int32, (8 * groups, slots), 0) == place
    picked = lax.dot_general(
        chosen.astype(bf16),
        rows[...].astype(bf16),
        (((0,), (0,)), ((), ())),
        preferred_element_type=f32,
    )
    flags = jnp.max(rows[:, flag_at : flag_at + 128], axis=0, keepdims=True)
    kept = picked[:, flag_at : flag_at + 128]
    flags = jnp.where(lax.axis_index("expert") >= first_narrow, jnp.broadcast_to(flags, kept.shape), kept)
    full = jnp.concatenate([picked[:, :flag_at], flags, picked[:, flag_at + 128 :]], axis=1)
    out[...] = full.astype(bf16).reshape(out.shape)


def pick_pieces(pieces, held, wanted, flag_at, first_narrow, cells):
    groups = pieces.shape[0]
    model = pieces.shape[1] * pieces.shape[2] // held
    slots, units, lanes = cells.shape
    row = model // lanes
    return pl.pallas_call(
        functools.partial(pick_kernel, held, flag_at, first_narrow),
        grid=(1,),
        in_specs=[whole((1, slots)), whole(pieces.shape), HBM],
        out_specs=pl.BlockSpec((slots, row, lanes), lambda i: (0, units // row - 1, 0)),
        out_shape=jax.ShapeDtypeStruct(cells.shape, bf16),
        input_output_aliases={2: 0},
        scratch_shapes=[pltpu.VMEM((8 * groups, model), f32)],
        compiler_params=params(ALL_MIB),
        name="adapter_pick",
    )(wanted.reshape(1, slots), pieces, cells)


def placement(ids, serving, places):
    tokens = ids.shape[1]
    mine, other = beside(serving)
    slots = mine.shape[0]
    below = lax.broadcasted_iota(jnp.int32, (slots, slots), 1) < lax.broadcasted_iota(
        jnp.int32, (slots, slots), 0
    )
    same = (mine == other).astype(f32)
    hot = jnp.sum(same, axis=1, keepdims=True) > 1.5
    second = jnp.sum(jnp.where(below, same, 0.0), axis=1, keepdims=True)
    named = mine[:, :tokens] == ids[0:1, :]
    for k in range(1, ids.shape[0]):
        named = named | (mine[:, :tokens] == ids[k : k + 1, :])
    before = lax.broadcasted_iota(jnp.int32, (tokens, tokens), 0) < lax.broadcasted_iota(
        jnp.int32, (tokens, tokens), 1
    )
    rank = jnp.dot(named.astype(bf16), before.astype(bf16), preferred_element_type=f32)
    rank = jnp.where(named, rank, -1.0)
    return [rank == jnp.where(hot, 2.0 * at + second, 1.0 * at) for at in places]


def dispatch_kernel(first, ids, serving, tokens, out, fills, sent, sems):
    places = fills.shape[0]
    slots, row, lanes = sent.shape[1:]
    masks = placement(ids[...], serving[...], range(first, first + places))
    for j in range(places):
        fills[j] = masks[j].astype(bf16)

    def send(j):
        return pltpu.make_async_copy(sent.at[j], out.at[:, tile_at(j, row), :], sems.at[j])

    @pl.loop(0, places)
    def _(j):
        part = jnp.dot(fills[j], tokens[...], preferred_element_type=f32).astype(bf16)
        sent[j] = part.reshape(slots, row, lanes)
        send(j).start()

    for j in range(places):
        send(j).wait()


def dispatch(ids, serving, tokens, first, places, spare):
    slots = serving.shape[1]
    count, model = tokens.shape
    row = model // 128
    return pl.pallas_call(
        functools.partial(dispatch_kernel, first),
        in_specs=[VMEM] * 3,
        out_specs=HBM,
        out_shape=jax.ShapeDtypeStruct((slots, (places + spare) * row, 128), bf16),
        scratch_shapes=[
            pltpu.VMEM((places, slots, count), bf16),
            pltpu.VMEM((places, slots, row, 128), bf16),
            pltpu.SemaphoreType.DMA((places,)),
        ],
        compiler_params=params(ALL_MIB),
        cost_estimate=pl.CostEstimate(
            flops=2 * places * slots * count * model,
            bytes_accessed=2 * places * slots * model,
            transcendentals=0,
        ),
        name="token_dispatch",
    )(ids, serving, tokens)


def expert_kernel(
    rank,
    factors_at,
    cells_hbm,
    factors_hbm,
    gate_hbm,
    up_hbm,
    down_hbm,
    out,
    cells,
    pieces,
    gate,
    up,
    down,
    x,
    factors,
    shrunk,
    hidden,
    sent,
    cell_sems,
    gate_sems,
    up_sems,
    down_sems,
    out_sems,
):
    slots = cells.shape[0]
    rows, model = x.shape
    units = hidden.shape[1]
    row = model // 128
    places = rows // slots
    tile = units // gate_sems.shape[0]
    width = sent.shape[2] * 128
    up_tiles, down_tiles = units // tile, model // width

    def load(i, source, target, size, sems):
        at = tile_at(i, size)
        return pltpu.make_async_copy(source.at[:, at], target.at[:, at], sems.at[i])

    def load_gate(i):
        return load(i, gate_hbm, gate, tile, gate_sems)

    def load_up(i):
        return load(i, up_hbm, up, tile, up_sems)

    def load_down(i):
        return load(i, down_hbm, down, width, down_sems)

    def send(i, j):
        at = pl.ds(pl.multiple_of(j * row + i * (width // 128), 8), width // 128)
        return pltpu.make_async_copy(sent.at[j], out.at[:, at, :], out_sems.at[i * places + j])

    def load_place(j):
        at = tile_at(j, row)
        return pltpu.make_async_copy(cells_hbm.at[:, at, :], cells.at[:, at, :], cell_sems.at[j])

    load_pieces = pltpu.make_async_copy(
        factors_hbm.at[:, pl.ds(factors_at * row, row), :], pieces, cell_sems.at[places]
    )
    load_pieces.start()
    for j in range(places):
        load_place(j).start()
    for i in range(up_tiles):
        load_gate(i).start()
        load_up(i).start()
    for i in range(down_tiles):
        load_down(i).start()

    load_pieces.wait()
    factors[...] = pieces[...].reshape(slots, model)

    @pl.loop(0, places)
    def _(j):
        here = tile_at(j, slots)
        load_place(j).wait()
        part = cells[:, tile_at(j, row), :].reshape(slots, model)
        x[here, :] = part
        shrunk[here, :] = lax.dot_general(
            part,
            factors[0 : 2 * rank, :],
            (((1,), (1,)), ((), ())),
            preferred_element_type=f32,
        ).astype(bf16)

    @pl.loop(0, up_tiles)
    def _(i):
        at = tile_at(i, tile)
        load_gate(i).wait()
        load_up(i).wait()
        into_gate = jnp.dot(x[...], gate[:, at], preferred_element_type=f32) + jnp.dot(
            shrunk[:, :rank], factors[3 * rank : 4 * rank, at], preferred_element_type=f32
        )
        up_at = pl.ds(pl.multiple_of(units + i * tile, tile), tile)
        into_up = jnp.dot(x[...], up[:, at], preferred_element_type=f32) + jnp.dot(
            shrunk[:, rank:], factors[3 * rank : 4 * rank, up_at], preferred_element_type=f32
        )
        hidden[:, at] = (into_gate / (1.0 + jnp.exp(-into_gate)) * into_up).astype(bf16)

    shrunk_down = lax.dot_general(
        hidden[...],
        factors[3 * rank : 4 * rank, 2 * units : 3 * units],
        (((1,), (1,)), ((), ())),
        preferred_element_type=f32,
    ).astype(bf16)

    @pl.loop(0, down_tiles)
    def _(i):
        at = tile_at(i, width)
        load_down(i).wait()
        total = jnp.dot(hidden[...], down[:, at], preferred_element_type=f32) + jnp.dot(
            shrunk_down, factors[2 * rank : 3 * rank, at], preferred_element_type=f32
        )
        for j in range(places):

            @pl.when(i > 0)
            def _():
                send(i - 1, j).wait()

            part = total[j * slots : (j + 1) * slots].astype(bf16)
            sent[j] = part.reshape(slots, width // 128, 128)
            send(i, j).start()

    for j in range(places):
        send(down_tiles - 1, j).wait()


def expert(cells, places, factors, factors_at, gate, up, down, rank):
    model, units = gate.shape
    slots = cells.shape[0]
    rows = slots * places
    row = model // 128
    tile, width = 256, 1024
    return pl.pallas_call(
        functools.partial(expert_kernel, rank, factors_at),
        in_specs=[HBM] * 5,
        out_specs=HBM,
        out_shape=jax.ShapeDtypeStruct((slots, places * row, 128), bf16),
        scratch_shapes=[
            pltpu.VMEM((slots, places * row, 128), bf16),
            pltpu.VMEM((slots, row, 128), bf16),
            pltpu.VMEM((model, units), bf16),
            pltpu.VMEM((model, units), bf16),
            pltpu.VMEM((units, model), bf16),
            pltpu.VMEM((rows, model), bf16),
            pltpu.VMEM((slots, model), bf16),
            pltpu.VMEM((rows, 2 * rank), bf16),
            pltpu.VMEM((rows, units), bf16),
            pltpu.VMEM((places, slots, width // 128, 128), bf16),
            pltpu.SemaphoreType.DMA((places + 1,)),
            pltpu.SemaphoreType.DMA((units // tile,)),
            pltpu.SemaphoreType.DMA((units // tile,)),
            pltpu.SemaphoreType.DMA((model // width,)),
            pltpu.SemaphoreType.DMA((places * (model // width),)),
        ],
        compiler_params=params(ALL_MIB),
        cost_estimate=pl.CostEstimate(
            flops=6 * rows * model * units,
            bytes_accessed=6 * model * units + 4 * rows * model,
            transcendentals=rows * units,
        ),
        name="slot_expert",
    )(cells, factors, gate, up, down)


def combine_kernel(first, ids, weight, serving, answers, *rest):
    sems, block, cells, out = rest[-1], rest[-2], rest[-3], rest[-4]
    count, model = out.shape
    rows, width = block.shape
    slots = cells.shape[0]
    places = rows // slots
    row = model // 128

    def load(i, j):
        at = pl.ds(pl.multiple_of(j * row + i * (width // 128), width // 128), width // 128)
        return pltpu.make_async_copy(answers.at[:, at, :], cells.at[:, at, :], sems.at[i * places + j])

    for i in range(model // width):
        for j in range(places):
            load(i, j).start()
    mine, _ = beside(serving[...])
    given = jnp.zeros((slots, count), f32)
    for k in range(ids.shape[0]):
        given = given + jnp.where(mine[:, :count] == ids[k : k + 1, :], weight[k : k + 1, :], 0.0)
    parts = []
    for mask in placement(ids[...], serving[...], range(first, first + places)):
        part = jnp.where(mask, given, 0.0)
        high = part.astype(bf16).astype(f32)
        parts.append(jnp.concatenate([high, part - high], axis=1).T)
    both = jnp.concatenate(parts, axis=1).astype(bf16)

    @pl.loop(0, model // width)
    def _(i):
        at = tile_at(i, width)
        for j in range(places):
            load(i, j).wait()
            units = pl.ds(pl.multiple_of(j * row + i * (width // 128), width // 128), width // 128)
            block[j * slots : (j + 1) * slots, :] = cells[:, units, :].reshape(slots, width)
        total = jnp.dot(both, block[...], preferred_element_type=f32)
        total = total[:count] + total[count:]
        if len(rest) == 5:
            total = total + rest[0][:, at]
        out[:, at] = total.astype(out.dtype)


def combine(ids, weight, serving, first, answers, model, before=None, kind=f32):
    count = ids.shape[1]
    slots, units, lanes = answers.shape

    places = units * lanes // model
    width = 2048
    more = () if before is None else (before,)
    return pl.pallas_call(
        functools.partial(combine_kernel, first),
        grid=(1,),
        in_specs=[VMEM] * 3 + [HBM] + [VMEM] * len(more),
        out_specs=whole((count, model)),
        out_shape=jax.ShapeDtypeStruct((count, model), kind),
        scratch_shapes=[
            pltpu.VMEM(answers.shape, bf16),
            pltpu.VMEM((places * slots, width), bf16),
            pltpu.SemaphoreType.DMA((places * (model // width),)),
        ],
        compiler_params=params(ALL_MIB),
        cost_estimate=pl.CostEstimate(
            flops=4 * count * places * slots * model,
            bytes_accessed=2 * places * slots * model,
            transcendentals=0,
        ),
        name="token_combine",
    )(ids, weight, serving, answers, *more)


def body(
    tokens,
    routed,
    weight,
    serving,
    gate,
    up,
    down,
    trainer_order,
    trainer_rows,
):
    groups = lax.axis_size("expert")
    dp_size = lax.axis_size("dp")
    slots = serving.shape[0]
    experts = trainer_order.shape[0]
    held, packed = trainer_rows.shape
    count, model = tokens.shape
    units = gate.shape[2]
    rank = packed // (3 * (model + units))
    first_narrow = 3 * rank // dp_size
    ids, weight, serving_row = routed.T, weight.T, serving.reshape(1, slots)

    def there(cells):
        return lax.all_to_all(cells, ("expert", "dp"), split_axis=0, concat_axis=0, tiled=True)

    mine = cut_pieces(
        trainer_rows, ids, serving_row, PLACES, groups, dp_size, model, units, rank
    )
    spread = lax.all_to_all(mine, "expert", split_axis=0, concat_axis=0, tiled=True)
    trainer_row = jnp.sum(
        jnp.where(
            serving[:, None] == trainer_order[None, :],
            jnp.arange(experts, dtype=jnp.int32)[None, :],
            0,
        ),
        axis=1,
    )
    sent = dispatch(ids, serving_row, tokens, 0, PLACES, 1)
    cells = there(pick_pieces(spread, held, trainer_row, 3 * units, first_narrow, sent))

    def answer(tokens_in, places):
        return there(expert(tokens_in, places, cells, PLACES, gate[0], up[0], down[0], rank))

    answers = answer(cells, PLACES)
    flags = cells[3 * rank :, PLACES * model // 128 + 3 * units // 128, 0]

    def one_round():
        return combine(ids, weight, serving_row, 0, answers, model, None, bf16)

    def two_rounds():
        total = combine(ids, weight, serving_row, 0, answers, model)
        places = MOST - PLACES
        more = there(dispatch(ids, serving_row, tokens, PLACES, places, 0))
        more = answer(more, places)
        return combine(ids, weight, serving_row, PLACES, more, model, total, bf16)

    return lax.cond(jnp.max(flags.astype(f32)) > 0.0, two_rounds, one_round)


def solution(mesh):
    split = P(("expert", "dp"), None)
    slot = P(("expert", "dp"), None, None)
    placed = (split, split, split, P(), slot, slot, slot, P(), P("expert", None))
    return jax.shard_map(body, mesh=mesh, in_specs=placed, out_specs=split, check_vma=False)
```

time: 219 us -> 212 us (0.968)
  local copies, waits for them, and re-layouts: 12.6 us -> 1.7 us
  waiting for transfers between devices: 64.6 us -> 67.9 us
    unnamed x19 -> x14, local copies, waits for them, and re-layouts: 11.6 us -> 1.7 us
    all_to_all x1, waiting for transfers between devices: 3.1 us -> 6.44 us  [body(): lax.all_to_all(mine, 'expert', split_axis=0, concat_axis=0, tiled=True)]
where the time goes in v3:
time: 212 us; the launch traced here: 211 us
  blocking collectives  82.5 us (39%)
  waiting for transfers between devices  67.9 us (32%)
  Pallas kernels  39.5 us (19%)
  starting transfers between devices  16 us (8%)
    all_to_all x1, blocking collectives, there(): lax.all_to_all(cells, ('expert', 'dp'), split_axis=0, concat_axis=0, tile...  82.5 us
    all_to_all x1, waiting for transfers between devices, there(): lax.all_to_all(cells, ('expert', 'dp'), split_axis=0, concat_axis=0, tile...  61.5 us
    pallas_call x1, Pallas kernels, expert(): pl.pallas_call(functools.partial(expert_kernel, rank, factors_at), in_spe...  24.9 us
    all_to_all x1, starting transfers between devices, there(): lax.all_to_all(cells, ('expert', 'dp'), split_axis=0, concat_axis=0, tile...  8.11 us
    all_to_all x1, starting transfers between devices, body(): lax.all_to_all(mine, 'expert', split_axis=0, concat_axis=0, tiled=True)  7.86 us
    all_to_all x1, waiting for transfers between devices, body(): lax.all_to_all(mine, 'expert', split_axis=0, concat_axis=0, tiled=True)  6.44 us
  transfers between devices with their start and end apart: 2, of which 2 were waited for; matrix products, arithmetic and copies ran while one was open for 1% of the time, Pallas kernels for 2%

profile of v3, /device:TPU:11, one launch (start us, length us, event | category | flops | bytes accessed | tf_op | source)
XLA Modules:
  0.0 210.6 jit_solution(14803836237925950100)
XLA Ops:
  0.0 0.0 copy-start.4
  0.0 0.0 copy-start.6
  0.0 0.0 copy-start.2
  0.0 0.0 copy-start.7
  0.0 3.2 %adapter_cut.1 = bf16[16,192,128]{2,1,0:T(8,128)(2,1)} custom-call(s32[8,64]{1,0:T(8,128)} %bitcast.16, s32[1,128]{1,0:T(1,128)} %bitcast.22, bf16[6,466944]{1,0:T(8,128)(2,1)} %rows.1), custom_call_target="tpu_custom_call" | custom-call | tf_op jit(solution)/shard_map/adapter_cut/pallas_call | solution.py:84
  3.2 7.9 %all-to-all-start.2 = ((bf16[16,192,128]{2,1,0:T(8,128)(2,1)}), bf16[16,192,128]{2,1,0:T(8,128)(2,1)S(1)}, u32[]{:S(2)}, u32[]{:S(2)}) async-start(bf16[16,192,128]{2,1,0:T(8,128)(2,1)} %adapter_cut.1), calls=%async_computation.2 | async-start | bytes 1572864 | tf_op jit(solution)/shard_map/all_to_all | solution.py:463
  11.1 0.0 copy-done.4
  11.1 0.0 copy-done.6
  11.1 0.0 copy-done.2
  11.1 4.1 %token_dispatch.3.cells = bf16[128,192,128]{2,1,0:T(8,128)(2,1)} custom-call(s32[8,64]{1,0:T(8,128)S(1)} %bitcast.17, s32[1,128]{1,0:T(1,128)S(1)} %bitcast.23, bf16[64,4096]{1,0:T(8,128)(2,1)S(1)} %copy-done.2), custom_call_target="tpu_custom_call" | custom-call | flops 335544320 | bytes 5242880 | tf_op jit(solution)/shard_map/token_dispatch/pallas_call | solution.py:184
  15.3 0.0 copy-done.7
  15.3 0.6 select_reduce_fusion
  15.9 6.4 %all-to-all-done.2.pieces = bf16[16,192,128]{2,1,0:T(8,128)(2,1)S(1)} async-done(((bf16[16,192,128]{2,1,0:T(8,128)(2,1)}), bf16[16,192,128]{2,1,0:T(8,128)(2,1)S(1)}, u32[]{:S(2)}, u32[]{:S(2)}) %all-to-all-start.2) | async-done | bytes 786464 | tf_op jit(solution)/shard_map/all_to_all | solution.py:463
  22.3 0.0 copy-start.1
  22.3 0.9 copy-done.1
  23.2 3.2 %adapter_pick.1 = bf16[128,192,128]{2,1,0:T(8,128)(2,1)} custom-call(s32[1,128]{1,0:T(1,128)} %bitcast.26, bf16[16,192,128]{2,1,0:T(8,128)(2,1)} %copy-done.1, bf16[128,192,128]{2,1,0:T(8,128)(2,1)} %token_dispatch.3.cells), custom_call_target="tpu_custom_call", output_to_operand_aliasing={{}: (2, {})} | custom-call | tf_op jit(solution)/shard_map/adapter_pick/pallas_call | solution.py:126
  26.4 82.5 %all_to_all.24.cells_hbm.factors_hbm = bf16[128,192,128]{2,1,0:T(8,128)(2,1)} all-to-all(bf16[128,192,128]{2,1,0:T(8,128)(2,1)} %adapter_pick.1), channel_id=1, replica_groups=mesh['expert'=16,'dp'=8] {'expert','dp'}, dimensions={0} | all-to-all | bytes 12582912 | tf_op jit(solution)/shard_map/all_to_all | solution.py:458
  108.9 24.9 %slot_expert.3 = bf16[128,160,128]{2,1,0:T(8,128)(2,1)} custom-call(bf16[128,192,128]{2,1,0:T(8,128)(2,1)} %all_to_all.24.cells_hbm.factors_hbm, bf16[128,192,128]{2,1,0:T(8,128)(2,1)} %all_to_all.24.cells_hbm.factors_hbm, bf16[4096,768]{1,0:T(8,128)(2,1)} %bitcast.10, bf16[4096,768]{1,0:T(8,128)(2,1)} %bitcast.12, bf16[768,4096]{1,0:T(8,128)(2,1)} %bitcast.14), custom_call_target="tpu_custom_call" | custom-call | flops 12079595520 | bytes 29360128 | tf_op jit(solution)/shard_map/slot_expert/pallas_call | solution.py:335
  133.7 0.0 copy-start.5
  133.7 8.1 %all-to-all-start.4 = ((bf16[128,160,128]{2,1,0:T(8,128)(2,1)}), bf16[128,160,128]{2,1,0:T(8,128)(2,1)}, u32[]{:S(2)}, u32[]{:S(2)}) async-start(bf16[128,160,128]{2,1,0:T(8,128)(2,1)} %slot_expert.3), calls=%async_computation.4 | async-start | bytes 10485760 | tf_op jit(solution)/shard_map/all_to_all | solution.py:458
  141.9 1.5 slice_reduce_fusion
  144.0 61.5 %all-to-all-done.4 = bf16[128,160,128]{2,1,0:T(8,128)(2,1)} async-done(((bf16[128,160,128]{2,1,0:T(8,128)(2,1)}), bf16[128,160,128]{2,1,0:T(8,128)(2,1)}, u32[]{:S(2)}, u32[]{:S(2)}) %all-to-all-start.4) | async-done | bytes 5242912 | tf_op jit(solution)/shard_map/all_to_all | solution.py:458
  205.5 0.0 copy-done.5
  205.5 4.3 %conditional.1 = (bf16[64,4096]{1,0:T(8,128)(2,1)S(1)}) conditional(s32[]{:T(128)} %convert_element_type.4, (s32[8,64]{1,0:T(8,128)S(1)}, f32[8,64]{1,0:T(8,128)S(1)}, s32[1,128]{1,0:T(1,128)S(1)}, bf16[128,160,128]{2,1,0:T(8,128)(2,1)}) %tuple.23, (s32[8,64]{1,0:T(8,128)S(1)}, s32[1,128]{1,0:T(1,128)S(1)}, bf16[64,4096]{1,0:T(8,128)(2,1)S(1)}, ...), branch_computations={%region_2.3_spmd, %region_3.4_spmd} | conditional | flops 8522825728 | bytes 65011780 | solution.py:491
  205.5 4.1 %token_combine.3 = bf16[64,4096]{1,0:T(8,128)(2,1)S(1)} custom-call(s32[8,64]{1,0:T(8,128)S(1)} %get-tuple-element.34.ids, f32[8,64]{1,0:T(8,128)S(1)} %get-tuple-element.35.weight, s32[1,128]{1,0:T(1,128)S(1)} %get-tuple-element.36.serving, bf16[128,160,128]{2,1,0:T(8,128)(2,1)} %get-tuple-element.37.answers), custom_call_target="tpu_custom_call" | custom-call | flops 671088640 | bytes 5242880 | tf_op jit(solution)/shard_map/cond/branch_0_fun/token_combine/pallas_call | solution.py:414
  209.8 0.0 copy-start.3
  209.8 0.8 copy-done.3
Async XLA Ops:
  0.0 11.1 %copy-start.4 = (s32[64,8]{0,1:T(8,128)S(1)}, s32[64,8]{0,1:T(8,128)}, u32[]{:S(2)}) copy-start(s32[64,8]{0,1:T(8,128)} %param.12) | copy-start | bytes 6148
  0.0 11.1 %copy-start.6 = (s32[128]{0:T(128)S(1)}, s32[128]{0:T(128)}, u32[]{:S(2)}) copy-start(s32[128]{0:T(128)} %param.14) | copy-start | bytes 1540
  0.0 11.1 %copy-start.2 = (bf16[64,4096]{1,0:T(8,128)(2,1)S(1)}, bf16[64,4096]{1,0:T(8,128)(2,1)}, u32[]{:S(2)}) copy-start(bf16[64,4096]{1,0:T(8,128)(2,1)} %tokens.1) | copy-start | bytes 1572868
  0.0 15.3 %copy-start.7 = (s32[96]{0:T(128)S(1)}, s32[96]{0:T(128)}, u32[]{:S(2)}) copy-start(s32[96]{0:T(128)} %param.18) | copy-start | bytes 1156
  3.2 19.1 %all-to-all-start.2 = ((bf16[16,192,128]{2,1,0:T(8,128)(2,1)}), bf16[16,192,128]{2,1,0:T(8,128)(2,1)S(1)}, u32[]{:S(2)}, u32[]{:S(2)}) async-start(bf16[16,192,128]{2,1,0:T(8,128)(2,1)} %adapter_cut.1), calls=%async_computation.2 | async-start | bytes 1572864 | tf_op jit(solution)/shard_map/all_to_all | solution.py:463
  22.3 0.9 copy-start.1
  133.7 71.7 %copy-start.5 = (f32[64,8]{0,1:T(8,128)S(1)}, f32[64,8]{0,1:T(8,128)}, u32[]{:S(2)}) copy-start(f32[64,8]{0,1:T(8,128)} %param.13) | copy-start | bytes 6148
  133.7 71.7 %all-to-all-start.4 = ((bf16[128,160,128]{2,1,0:T(8,128)(2,1)}), bf16[128,160,128]{2,1,0:T(8,128)(2,1)}, u32[]{:S(2)}, u32[]{:S(2)}) async-start(bf16[128,160,128]{2,1,0:T(8,128)(2,1)} %slot_expert.3), calls=%async_computation.4 | async-start | bytes 10485760 | tf_op jit(solution)/shard_map/all_to_all | solution.py:458
  209.8 0.8 copy-start.3

commit v4 on v3

--- a/solution.py
+++ b/solution.py
@@ -9,8 +9,8 @@
 
 bf16 = jnp.bfloat16
 f32 = jnp.float32
-MIB = 1 << 20
-ALL_MIB = 60
+ALL_BYTES = 63_400_000
+MOST_BYTES = 55 << 20
 
 PLACES = 5
 MOST = 8
@@ -19,8 +19,8 @@
 HBM = pl.BlockSpec(memory_space=pltpu.HBM)
 
 
-def params(limit_mib):
-    return pltpu.CompilerParams(vmem_limit_bytes=limit_mib * MIB)
+def params(limit):
+    return pltpu.CompilerParams(vmem_limit_bytes=limit)
 
 
 def whole(shape):
@@ -36,12 +36,13 @@
     return across.T, across
 
 
-def cut_kernel(wide_rows, narrow, dp_size, limit, ids, serving, rows, out, cut, sems):
+def cut_kernel(wide_rows, narrow, dp_size, limit, ids, serving, rows, out, cut, flat, sems, out_sems):
     groups, held, model = cut.shape
     dp_index = lax.axis_index("dp")
     first_narrow = wide_rows // dp_size
     rank = wide_rows // 3
     copies = []
+    owners = []
     for e in range(groups):
         piece = e * dp_size + dp_index
         if e < first_narrow:
@@ -52,6 +53,7 @@
                 (wide_rows * model + (g * rank + q) * narrow, g * narrow, narrow) for g in range(3)
             ]
         for source, target, width in spans:
+            owners.append(e)
             copies.append(
                 pltpu.make_async_copy(
                     rows.at[:, pl.ds(pl.multiple_of(source, 128), width)],
@@ -71,10 +73,16 @@
     over = jnp.max(over, axis=0, keepdims=True)
     for e in range(first_narrow, groups):
         cut[e, :, 3 * narrow :] = jnp.broadcast_to(over, (held, model - 3 * narrow)).astype(bf16)
-    for copy in copies:
-        copy.wait()
+    sends = []
     for e in range(groups):
-        out[e] = cut[e].reshape(out.shape[1:])
+        for copy, owner in zip(copies, owners):
+            if owner == e:
+                copy.wait()
+        flat[e] = cut[e].reshape(flat.shape[1:])
+        sends.append(pltpu.make_async_copy(flat.at[e], out.at[e], out_sems.at[e]))
+        sends[e].start()
+    for send in sends:
+        send.wait()
 
 
 def cut_pieces(rows, ids, serving, limit, groups, dp_size, model, narrow, rank):
@@ -84,54 +92,75 @@
     return pl.pallas_call(
         functools.partial(cut_kernel, wide_rows, narrow, dp_size, limit),
         in_specs=[VMEM, VMEM, HBM],
-        out_specs=VMEM,
+        out_specs=HBM,
         out_shape=jax.ShapeDtypeStruct((groups, held * model // 128, 128), bf16),
         scratch_shapes=[
             pltpu.VMEM((groups, held, model), bf16),
+            pltpu.VMEM((groups, held * model // 128, 128), bf16),
             pltpu.SemaphoreType.DMA((first_narrow + 3 * (groups - first_narrow),)),
+            pltpu.SemaphoreType.DMA((groups,)),
         ],
-        compiler_params=params(ALL_MIB),
+        compiler_params=params(ALL_BYTES),
         name="adapter_cut",
     )(ids, serving, rows)
 
 
-def pick_kernel(held, flag_at, first_narrow, wanted, pieces, cells, out, rows):
+def pick_kernel(held, flag_at, first_narrow, wanted, pieces, cells, out, rows, sent, sems):
     groups = pieces.shape[0]
     model = rows.shape[1]
-    slots = out.shape[0]
+    slots = sent.shape[1]
     rows[...] = jnp.zeros_like(rows)
     for e in range(groups):
         rows[8 * e : 8 * e + held, :] = pieces[e].reshape(held, model).astype(f32)
     want = wanted[...]
     place = (want // held) * 8 + want % held
     chosen = lax.broadcasted_iota(jnp.int32, (8 * groups, slots), 0) == place
-    picked = lax.dot_general(
-        chosen.astype(bf16),
-        rows[...].astype(bf16),
-        (((0,), (0,)), ((), ())),
-        preferred_element_type=f32,
-    )
-    flags = jnp.max(rows[:, flag_at : flag_at + 128], axis=0, keepdims=True)
-    kept = picked[:, flag_at : flag_at + 128]
-    flags = jnp.where(lax.axis_index("expert") >= first_narrow, jnp.broadcast_to(flags, kept.shape), kept)
-    full = jnp.concatenate([picked[:, :flag_at], flags, picked[:, flag_at + 128 :]], axis=1)
-    out[...] = full.astype(bf16).reshape(out.shape)
+    chosen = chosen.astype(bf16)
+    parts = sems.shape[0]
+    width = model // parts
+    copies = []
+    for c in range(parts):
+        part = rows[:, c * width : (c + 1) * width]
+        picked = lax.dot_general(
+            chosen,
+            part.astype(bf16),
+            (((0,), (0,)), ((), ())),
+            preferred_element_type=f32,
+        )
+        if flag_at // width == c:
+            at = flag_at % width
+            flags = jnp.max(part[:, at : at + 128], axis=0, keepdims=True)
+            kept = picked[:, at : at + 128]
+            flags = jnp.where(
+                lax.axis_index("expert") >= first_narrow, jnp.broadcast_to(flags, kept.shape), kept
+            )
+            picked = jnp.concatenate([picked[:, :at], flags, picked[:, at + 128 :]], axis=1)
+        sent[c] = picked.astype(bf16).reshape(sent.shape[1:])
+        at = out.shape[1] - (parts - c) * (width // 128)
+        copies.append(
+            pltpu.make_async_copy(sent.at[c], out.at[:, pl.ds(at, width // 128), :], sems.at[c])
+        )
+        copies[c].start()
+    for copy in copies:
+        copy.wait()
 
 
 def pick_pieces(pieces, held, wanted, flag_at, first_narrow, cells):
     groups = pieces.shape[0]
     model = pieces.shape[1] * pieces.shape[2] // held
-    slots, units, lanes = cells.shape
-    row = model // lanes
+    slots, _, lanes = cells.shape
     return pl.pallas_call(
         functools.partial(pick_kernel, held, flag_at, first_narrow),
-        grid=(1,),
-        in_specs=[whole((1, slots)), whole(pieces.shape), HBM],
-        out_specs=pl.BlockSpec((slots, row, lanes), lambda i: (0, units // row - 1, 0)),
+        in_specs=[VMEM, VMEM, HBM],
+        out_specs=HBM,
         out_shape=jax.ShapeDtypeStruct(cells.shape, bf16),
         input_output_aliases={2: 0},
-        scratch_shapes=[pltpu.VMEM((8 * groups, model), f32)],
-        compiler_params=params(ALL_MIB),
+        scratch_shapes=[
+            pltpu.VMEM((8 * groups, model), f32),
+            pltpu.VMEM((4, slots, model // 4 // lanes, lanes), bf16),
+            pltpu.SemaphoreType.DMA((4,)),
+        ],
+        compiler_params=params(MOST_BYTES),
         name="adapter_pick",
     )(wanted.reshape(1, slots), pieces, cells)
 
@@ -191,7 +220,7 @@
             pltpu.VMEM((places, slots, row, 128), bf16),
             pltpu.SemaphoreType.DMA((places,)),
         ],
-        compiler_params=params(ALL_MIB),
+        compiler_params=params(ALL_BYTES),
         cost_estimate=pl.CostEstimate(
             flops=2 * places * slots * count * model,
             bytes_accessed=2 * places * slots * model,
@@ -354,7 +383,7 @@
             pltpu.SemaphoreType.DMA((model // width,)),
             pltpu.SemaphoreType.DMA((places * (model // width),)),
         ],
-        compiler_params=params(ALL_MIB),
+        compiler_params=params(ALL_BYTES),
         cost_estimate=pl.CostEstimate(
             flops=6 * rows * model * units,
             bytes_accessed=6 * model * units + 4 * rows * model,
@@ -364,21 +393,9 @@
     )(cells, factors, gate, up, down)
 
 
-def combine_kernel(first, ids, weight, serving, answers, *rest):
-    sems, block, cells, out = rest[-1], rest[-2], rest[-3], rest[-4]
-    count, model = out.shape
-    rows, width = block.shape
-    slots = cells.shape[0]
-    places = rows // slots
-    row = model // 128
-
-    def load(i, j):
-        at = pl.ds(pl.multiple_of(j * row + i * (width // 128), width // 128), width // 128)
-        return pltpu.make_async_copy(answers.at[:, at, :], cells.at[:, at, :], sems.at[i * places + j])
-
-    for i in range(model // width):
-        for j in range(places):
-            load(i, j).start()
+def weights_kernel(first, ids, weight, serving, after, out):
+    slots, count = serving.shape[1], ids.shape[1]
+    places = out.shape[1] // slots
     mine, _ = beside(serving[...])
     given = jnp.zeros((slots, count), f32)
     for k in range(ids.shape[0]):
@@ -388,7 +405,35 @@
         part = jnp.where(mask, given, 0.0)
         high = part.astype(bf16).astype(f32)
         parts.append(jnp.concatenate([high, part - high], axis=1).T)
-    both = jnp.concatenate(parts, axis=1).astype(bf16)
+    out[...] = jnp.concatenate(parts, axis=1).astype(bf16)
+
+
+def combine_weights(ids, weight, serving, first, places, after):
+    shape = (2 * ids.shape[1], places * serving.shape[1])
+    return pl.pallas_call(
+        functools.partial(weights_kernel, first),
+        in_specs=[VMEM] * 3 + [HBM],
+        out_specs=VMEM,
+        out_shape=jax.ShapeDtypeStruct(shape, bf16),
+        name="combine_weights",
+    )(ids, weight, serving, after)
+
+
+def combine_kernel(both, answers, *rest):
+    sems, block, cells, out = rest[-1], rest[-2], rest[-3], rest[-4]
+    count, model = out.shape
+    rows, width = block.shape
+    slots = cells.shape[0]
+    places = rows // slots
+    row = model // 128
+
+    def load(i, j):
+        at = pl.ds(pl.multiple_of(j * row + i * (width // 128), width // 128), width // 128)
+        return pltpu.make_async_copy(answers.at[:, at, :], cells.at[:, at, :], sems.at[i * places + j])
+
+    for i in range(model // width):
+        for j in range(places):
+            load(i, j).start()
 
     @pl.loop(0, model // width)
     def _(i):
@@ -397,24 +442,24 @@
             load(i, j).wait()
             units = pl.ds(pl.multiple_of(j * row + i * (width // 128), width // 128), width // 128)
             block[j * slots : (j + 1) * slots, :] = cells[:, units, :].reshape(slots, width)
-        total = jnp.dot(both, block[...], preferred_element_type=f32)
+        total = jnp.dot(both[...], block[...], preferred_element_type=f32)
         total = total[:count] + total[count:]
         if len(rest) == 5:
             total = total + rest[0][:, at]
         out[:, at] = total.astype(out.dtype)
 
 
-def combine(ids, weight, serving, first, answers, model, before=None, kind=f32):
-    count = ids.shape[1]
+def combine(both, answers, model, before=None, kind=f32):
+    count = both.shape[0] // 2
     slots, units, lanes = answers.shape
 
     places = units * lanes // model
     width = 2048
     more = () if before is None else (before,)
     return pl.pallas_call(
-        functools.partial(combine_kernel, first),
+        combine_kernel,
         grid=(1,),
-        in_specs=[VMEM] * 3 + [HBM] + [VMEM] * len(more),
+        in_specs=[VMEM, HBM] + [VMEM] * len(more),
         out_specs=whole((count, model)),
         out_shape=jax.ShapeDtypeStruct((count, model), kind),
         scratch_shapes=[
@@ -422,14 +467,14 @@
             pltpu.VMEM((places * slots, width), bf16),
             pltpu.SemaphoreType.DMA((places * (model // width),)),
         ],
-        compiler_params=params(ALL_MIB),
+        compiler_params=params(ALL_BYTES),
         cost_estimate=pl.CostEstimate(
             flops=4 * count * places * slots * model,
             bytes_accessed=2 * places * slots * model,
             transcendentals=0,
         ),
         name="token_combine",
-    )(ids, weight, serving, answers, *more)
+    )(both, answers, *more)
 
 
 def body(
@@ -478,15 +523,18 @@
     answers = answer(cells, PLACES)
     flags = cells[3 * rank :, PLACES * model // 128 + 3 * units // 128, 0]
 
+    both = combine_weights(ids, weight, serving_row, 0, PLACES, cells)
+
     def one_round():
-        return combine(ids, weight, serving_row, 0, answers, model, None, bf16)
+        return combine(both, answers, model, None, bf16)
 
     def two_rounds():
-        total = combine(ids, weight, serving_row, 0, answers, model)
+        total = combine(both, answers, model)
         places = MOST - PLACES
         more = there(dispatch(ids, serving_row, tokens, PLACES, places, 0))
         more = answer(more, places)
-        return combine(ids, weight, serving_row, PLACES, more, model, total, bf16)
+        after = combine_weights(ids, weight, serving_row, PLACES, places, more)
+        return combine(after, more, model, total, bf16)
 
     return lax.cond(jnp.max(flags.astype(f32)) > 0.0, two_rounds, one_round)
 

time: 212 us -> 212 us (level)
    pallas_call x1 -> x2, Pallas kernels: 4.11 us -> 4.53 us  [the longest x1 4.08 us: combine(): pl.pallas_call(combine_kernel, grid=(1,), in_specs=[VMEM, HBM] + [VMEM] *...]
where the time goes in v4:
time: 212 us; the launch traced here: 210 us
  blocking collectives  82.5 us (39%)
  waiting for transfers between devices  67.4 us (32%)
  Pallas kernels  39.4 us (19%)
  starting transfers between devices  16 us (8%)
    all_to_all x1, blocking collectives, there(): lax.all_to_all(cells, ('expert', 'dp'), split_axis=0, concat_axis=0, tile...  82.5 us
    all_to_all x1, waiting for transfers between devices, there(): lax.all_to_all(cells, ('expert', 'dp'), split_axis=0, concat_axis=0, tile...  61 us
    pallas_call x1, Pallas kernels, expert(): pl.pallas_call(functools.partial(expert_kernel, rank, factors_at), in_spe...  24.9 us
    all_to_all x1, starting transfers between devices, there(): lax.all_to_all(cells, ('expert', 'dp'), split_axis=0, concat_axis=0, tile...  8.1 us
    all_to_all x1, starting transfers between devices, body(): lax.all_to_all(mine, 'expert', split_axis=0, concat_axis=0, tiled=True)  7.86 us
    all_to_all x1, waiting for transfers between devices, body(): lax.all_to_all(mine, 'expert', split_axis=0, concat_axis=0, tiled=True)  6.43 us
  transfers between devices with their start and end apart: 2, of which 2 were waited for; matrix products, arithmetic and copies ran while one was open for 1% of the time, Pallas kernels for 2%

profile of v4, /device:TPU:11, one launch (start us, length us, event | category | flops | bytes accessed | tf_op | source)
XLA Modules:
  0.0 210.1 jit_solution(17522380530537563019)
XLA Ops:
  0.0 0.0 copy-start.4
  0.0 0.0 copy-start.6
  0.0 0.0 copy-start.2
  0.0 0.0 copy-start.7
  0.0 3.0 %adapter_cut.1 = bf16[16,192,128]{2,1,0:T(8,128)(2,1)} custom-call(s32[8,64]{1,0:T(8,128)} %bitcast.16, s32[1,128]{1,0:T(1,128)} %bitcast.22, bf16[6,466944]{1,0:T(8,128)(2,1)} %rows.1), custom_call_target="tpu_custom_call" | custom-call | tf_op jit(solution)/shard_map/adapter_cut/pallas_call | solution.py:92
  3.0 7.9 %all-to-all-start.2 = ((bf16[16,192,128]{2,1,0:T(8,128)(2,1)}), bf16[16,192,128]{2,1,0:T(8,128)(2,1)S(1)}, u32[]{:S(2)}, u32[]{:S(2)}) async-start(bf16[16,192,128]{2,1,0:T(8,128)(2,1)} %adapter_cut.1), calls=%async_computation.2 | async-start | bytes 1572864 | tf_op jit(solution)/shard_map/all_to_all | solution.py:508
  10.9 0.0 copy-done.4
  10.9 0.0 copy-done.6
  10.9 0.0 copy-done.2
  10.9 4.1 %token_dispatch.3.cells = bf16[128,192,128]{2,1,0:T(8,128)(2,1)} custom-call(s32[8,64]{1,0:T(8,128)S(1)} %bitcast.17, s32[1,128]{1,0:T(1,128)S(1)} %bitcast.23, bf16[64,4096]{1,0:T(8,128)(2,1)S(1)} %copy-done.2), custom_call_target="tpu_custom_call" | custom-call | flops 335544320 | bytes 5242880 | tf_op jit(solution)/shard_map/token_dispatch/pallas_call | solution.py:213
  15.0 0.0 copy-done.7
  15.1 0.6 select_reduce_fusion
  15.7 6.4 %all-to-all-done.2.pieces = bf16[16,192,128]{2,1,0:T(8,128)(2,1)S(1)} async-done(((bf16[16,192,128]{2,1,0:T(8,128)(2,1)}), bf16[16,192,128]{2,1,0:T(8,128)(2,1)S(1)}, u32[]{:S(2)}, u32[]{:S(2)}) %all-to-all-start.2) | async-done | bytes 786464 | tf_op jit(solution)/shard_map/all_to_all | solution.py:508
  22.1 0.0 copy-start.1
  22.1 0.9 copy-done.1
  23.0 2.9 %adapter_pick.1 = bf16[128,192,128]{2,1,0:T(8,128)(2,1)} custom-call(s32[1,128]{1,0:T(1,128)} %bitcast.26, bf16[16,192,128]{2,1,0:T(8,128)(2,1)} %copy-done.1, bf16[128,192,128]{2,1,0:T(8,128)(2,1)} %token_dispatch.3.cells), custom_call_target="tpu_custom_call", output_to_operand_aliasing={{}: (2, {})} | custom-call | tf_op jit(solution)/shard_map/adapter_pick/pallas_call | solution.py:152
  25.9 82.5 %all_to_all.24.after.cells_hbm.factors_hbm = bf16[128,192,128]{2,1,0:T(8,128)(2,1)} all-to-all(bf16[128,192,128]{2,1,0:T(8,128)(2,1)} %adapter_pick.1), channel_id=1, replica_groups=mesh['expert'=16,'dp'=8] {'expert','dp'}, dimensions={0} | all-to-all | bytes 12582912 | tf_op jit(solution)/shard_map/all_to_all | solution.py:503
  108.4 24.9 %slot_expert.3 = bf16[128,160,128]{2,1,0:T(8,128)(2,1)} custom-call(bf16[128,192,128]{2,1,0:T(8,128)(2,1)} %all_to_all.24.after.cells_hbm.factors_hbm, bf16[128,192,128]{2,1,0:T(8,128)(2,1)} %all_to_all.24.after.cells_hbm.factors_hbm, bf16[4096,768]{1,0:T(8,128)(2,1)} %bitcast.10, bf16[4096,768]{1,0:T(8,128)(2,1)} %bitcast.12, bf16[768,4096]{1,0:T(8,128)(2,1)} %bitcast.14), custom_call_target="tpu_custom_call" | custom-call | flops 12079595520 | bytes 29360128 | tf_op jit(solution)/shard_map/slot_expert/pallas_call | solution.py:364
  133.3 0.0 copy-start.5
  133.3 8.1 %all-to-all-start.4 = ((bf16[128,160,128]{2,1,0:T(8,128)(2,1)}), bf16[128,160,128]{2,1,0:T(8,128)(2,1)}, u32[]{:S(2)}, u32[]{:S(2)}) async-start(bf16[128,160,128]{2,1,0:T(8,128)(2,1)} %slot_expert.3), calls=%async_computation.4 | async-start | bytes 10485760 | tf_op jit(solution)/shard_map/all_to_all | solution.py:503
  141.4 1.5 slice_reduce_fusion
  143.5 0.0 copy-done.5
  143.5 0.4 combine_weights.3
  144.0 61.0 %all-to-all-done.4 = bf16[128,160,128]{2,1,0:T(8,128)(2,1)} async-done(((bf16[128,160,128]{2,1,0:T(8,128)(2,1)}), bf16[128,160,128]{2,1,0:T(8,128)(2,1)}, u32[]{:S(2)}, u32[]{:S(2)}) %all-to-all-start.4) | async-done | bytes 5242912 | tf_op jit(solution)/shard_map/all_to_all | solution.py:503
  205.0 4.3 %conditional.1 = (bf16[64,4096]{1,0:T(8,128)(2,1)S(1)}) conditional(s32[]{:T(128)} %convert_element_type.4, (bf16[128,640]{1,0:T(8,128)(2,1)S(1)}, bf16[128,160,128]{2,1,0:T(8,128)(2,1)}) %tuple.11, (s32[8,64]{1,0:T(8,128)S(1)}, s32[1,128]{1,0:T(1,128)S(1)}, bf16[64,4096]{1,0:T(8,128)(2,1)S(1)}, bf16[1,4096,768]{2,1,0:T(8,128)(2,1)}, ...), branch_computations={%region_2.3_spmd, %region_3.4_spmd} | conditional | flops 8522825728 | bytes 65011780 | solution.py:539
  205.0 4.1 %token_combine.3 = bf16[64,4096]{1,0:T(8,128)(2,1)S(1)} custom-call(bf16[128,640]{1,0:T(8,128)(2,1)S(1)} %get-tuple-element.32.both, bf16[128,160,128]{2,1,0:T(8,128)(2,1)} %get-tuple-element.33.answers), custom_call_target="tpu_custom_call" | custom-call | flops 671088640 | bytes 5242880 | tf_op jit(solution)/shard_map/cond/branch_0_fun/token_combine/pallas_call | solution.py:459
  209.3 0.0 copy-start.3
  209.3 0.8 copy-done.3
Async XLA Ops:
  0.0 10.9 %copy-start.4 = (s32[64,8]{0,1:T(8,128)S(1)}, s32[64,8]{0,1:T(8,128)}, u32[]{:S(2)}) copy-start(s32[64,8]{0,1:T(8,128)} %param.12) | copy-start | bytes 6148
  0.0 10.9 %copy-start.6 = (s32[128]{0:T(128)S(1)}, s32[128]{0:T(128)}, u32[]{:S(2)}) copy-start(s32[128]{0:T(128)} %param.14) | copy-start | bytes 1540
  0.0 10.9 %copy-start.2 = (bf16[64,4096]{1,0:T(8,128)(2,1)S(1)}, bf16[64,4096]{1,0:T(8,128)(2,1)}, u32[]{:S(2)}) copy-start(bf16[64,4096]{1,0:T(8,128)(2,1)} %tokens.1) | copy-start | bytes 1572868
  0.0 15.0 %copy-start.7 = (s32[96]{0:T(128)S(1)}, s32[96]{0:T(128)}, u32[]{:S(2)}) copy-start(s32[96]{0:T(128)} %param.18) | copy-start | bytes 1156
  3.0 19.1 %all-to-all-start.2 = ((bf16[16,192,128]{2,1,0:T(8,128)(2,1)}), bf16[16,192,128]{2,1,0:T(8,128)(2,1)S(1)}, u32[]{:S(2)}, u32[]{:S(2)}) async-start(bf16[16,192,128]{2,1,0:T(8,128)(2,1)} %adapter_cut.1), calls=%async_computation.2 | async-start | bytes 1572864 | tf_op jit(solution)/shard_map/all_to_all | solution.py:508
  22.1 0.9 copy-start.1
  133.3 10.3 %copy-start.5 = (f32[64,8]{0,1:T(8,128)S(1)}, f32[64,8]{0,1:T(8,128)}, u32[]{:S(2)}) copy-start(f32[64,8]{0,1:T(8,128)} %param.13) | copy-start | bytes 6148
  133.3 71.7 %all-to-all-start.4 = ((bf16[128,160,128]{2,1,0:T(8,128)(2,1)}), bf16[128,160,128]{2,1,0:T(8,128)(2,1)}, u32[]{:S(2)}, u32[]{:S(2)}) async-start(bf16[128,160,128]{2,1,0:T(8,128)(2,1)} %slot_expert.3), calls=%async_computation.4 | async-start | bytes 10485760 | tf_op jit(solution)/shard_map/all_to_all | solution.py:503
  209.3 0.8 copy-start.3
